TPU v7x, 512 devices: a whole 4x4x16 slice. The times are simulated.
512 devices in a mesh: tile: 32 (over z, y_lo), member: 16 (over y_hi, x, core).
Axes of the slice: x: 4, y: 4 (y_hi: 2, y_lo: 2; y = y_hi * 2 + y_lo), z: 16, core: 2. Of those that a mesh axis runs over, the one named last changes fastest.
Arguments:
- perturbations: bfloat16 [32, 6, 512, 512], P('member', None, 'tile'), may hold values from -6 to 6
- control: float32 [6, 512, 512], P(None, 'tile'), may hold values from -6 to 6
- band_rows: float32 [512, 25], P('tile'), may hold values from 0.5 to 2
- band_cols: float32 [512, 25], replicated, may hold values from 0.5 to 2
- edge_peer: int32 [6, 4], replicated, may hold values from 0 to 23, as said below
- edge_flip: int32 [6, 4], replicated, may hold values from 0 to 1, as said below
Outputs:
- increment: float32 [6, 512, 512], P(None, 'tile')
Inputs may be any that keep to these rules, and one draw needn't show every extreme that they name: The faces are those of a cube: edge_peer pairs the 24 face edges two by two (the neighbour of the neighbour is the edge itself, never on the same face), and cells line up one to one along each shared edge. `edge_flip`: equal on both sides of each shared edge.
All inputs are finite; a program needn't handle non-finite values.
Results may differ from a plain program's by a relative error of at most 0.0033.
Values may be sent and summed in bfloat16 or wider, within the bound.
A program may use at most 64 MiB of HBM per device.

v0:
```python
import jax
import jax.numpy as jnp
from jax import lax
from jax.sharding import PartitionSpec as P


def spread_2(value, axis, source):
    kept = jnp.where(lax.axis_index(axis) == source, value, 0).astype(value.dtype)
    return lax.psum(kept, axis)


def from_partner(value, axis, distance):
    return lax.ppermute(value, axis, [(i, i ^ 1 << distance) for i in range(lax.axis_size(axis))])


def padded_2(value, sides, width):
    for axis, dim in sides:
        size, length = (lax.axis_size(axis), value.shape[dim])
        up = [(i, (i + 1) % size) for i in range(size - 1)]
        down = [(j, i) for i, j in up]
        last = lax.slice_in_dim(value, length - width, length, axis=dim)
        initial = lax.slice_in_dim(value, 0, width, axis=dim)
        before = lax.ppermute(last, axis, up)
        after = lax.ppermute(initial, axis, down)
        value = jnp.concatenate([before, value, after], axis=dim)
    return value


def filter_taps(band, half_width):
    tap_count = 2 * half_width + 1
    offsets = jnp.arange(tap_count, dtype=jnp.float32) - half_width
    taper_curve = jnp.exp(-((offsets / half_width) ** 2))
    normalizer = 1.0 / jnp.sqrt(jnp.sqrt(jnp.sum(taper_curve * taper_curve)) * jnp.sum(taper_curve))
    return (band * (taper_curve * normalizer)[None, :]).astype(jnp.bfloat16)


def row_matrix(taps_rows, half_width):
    row_count, tap_count = taps_rows.shape
    out_index = jnp.arange(row_count)[:, None, None]
    in_index = jnp.arange(row_count + 2 * half_width)[None, :, None]
    offsets = jnp.arange(tap_count)[None, None, :]
    onehot = (in_index - out_index == offsets).astype(jnp.float32)
    return jnp.einsum("rk,rck->rc", taps_rows.astype(jnp.float32), onehot).astype(jnp.bfloat16)


def band_blocks(taps_cols, col_block):
    edge_cells, tap_count = taps_cols.shape
    block_count = edge_cells // col_block
    in_index = jnp.arange(col_block + tap_count - 1)[:, None, None]
    out_index = jnp.arange(col_block)[None, :, None]
    offsets = jnp.arange(tap_count)[None, None, :]
    onehot = (in_index - out_index == offsets).astype(jnp.float32)
    grouped = taps_cols.astype(jnp.float32).reshape(block_count, col_block, tap_count)
    return jnp.einsum("bjk,cjk->bcj", grouped, onehot).astype(jnp.bfloat16)


def apply_cols(padded, blocks):
    block_count, span, col_block = blocks.shape
    windows = jnp.stack(
        [padded[..., index * col_block : index * col_block + span] for index in range(block_count)],
        axis=0,
    )
    result = jnp.einsum("bmfrc,bcj->mfrbj", windows, blocks, preferred_element_type=jnp.float32)
    return result.reshape(result.shape[:3] + (block_count * col_block,))


def apply_cols_adjoint(field, blocks):
    block_count, span, col_block = blocks.shape
    grouped = field.reshape(field.shape[:3] + (block_count, col_block))
    partials = jnp.einsum("mfrbj,bcj->bmfrc", grouped, blocks, preferred_element_type=jnp.float32)
    spread = jnp.zeros(field.shape[:3] + (block_count * col_block + span - col_block,), jnp.float32)
    for index in range(block_count):
        spread = spread.at[..., index * col_block : index * col_block + span].add(partials[index])
    return spread


def column_strips(field, half_width):
    edge_cells = field.shape[-1]
    left_side = jnp.swapaxes(field[..., :half_width], -1, -2)
    right_side = jnp.swapaxes(field[..., edge_cells - half_width :][..., ::-1], -1, -2)
    return jnp.stack([left_side, right_side], axis=2)


def face_rows(top_strip, bottom_strip):
    last_index = lax.axis_size("tile") - 1
    spread = []
    for root_index, strips in ((0, top_strip), (last_index, bottom_strip)):
        spread.append(spread_2(strips, "tile", root_index))
    return (spread[0], spread[1])


def face_columns(col_strips):
    return lax.all_gather(col_strips, "tile", axis=4, tiled=True)


def spread_columns(col_strips, need_whole):
    swapped = col_strips
    for bit_index in range(lax.axis_size("tile").bit_length() - 1):
        swapped = from_partner(swapped, "tile", bit_index)
    mirrored = swapped[..., ::-1]
    whole_cols = face_columns(col_strips) if need_whole else None
    return (mirrored, whole_cols)


def column_targets(edge_peer, edge_flip, tile_rank, top_all, bottom_all, col_strips, mirrored):
    member_count, face_count, half_width, row_count = (
        col_strips.shape[0],
        col_strips.shape[1],
        col_strips.shape[3],
        col_strips.shape[4],
    )
    edge_cells = top_all.shape[-1]
    start_here = tile_rank * row_count
    start_there = edge_cells - (tile_rank + 1) * row_count
    top_here = lax.dynamic_slice_in_dim(top_all, start_here, row_count, 3)
    bottom_here = lax.dynamic_slice_in_dim(bottom_all, start_here, row_count, 3)
    top_there = lax.dynamic_slice_in_dim(top_all, start_there, row_count, 3)[..., ::-1]
    bottom_there = lax.dynamic_slice_in_dim(bottom_all, start_there, row_count, 3)[..., ::-1]
    direct = jnp.stack([top_here, bottom_here, col_strips[:, :, 0], col_strips[:, :, 1]], axis=2)
    opposite = jnp.stack([top_there, bottom_there, mirrored[:, :, 0], mirrored[:, :, 1]], axis=2)
    direct = direct.reshape(member_count, face_count * 4, half_width, row_count)
    opposite = opposite.reshape(member_count, face_count * 4, half_width, row_count)
    source_codes = edge_peer[:, 2:].reshape(-1)
    turned = edge_flip[:, 2:].reshape(-1)
    picked = jnp.where(
        turned[None, :, None, None] == 1,
        jnp.take(opposite, source_codes, axis=1),
        jnp.take(direct, source_codes, axis=1),
    )
    return picked.reshape(member_count, face_count, 2, half_width, row_count)


def row_targets(edge_peer, edge_flip, top_all, bottom_all, whole_cols):
    member_count, face_count, half_width, edge_cells = top_all.shape
    candidates = jnp.stack([top_all, bottom_all, whole_cols[:, :, 0], whole_cols[:, :, 1]], axis=2)
    candidates = candidates.reshape(member_count, face_count * 4, half_width, edge_cells)
    picked = jnp.take(candidates, edge_peer[:, :2].reshape(-1), axis=1)
    turned = edge_flip[:, :2].reshape(-1)
    picked = jnp.where(turned[None, :, None, None] == 1, picked[..., ::-1], picked)
    return picked.reshape(member_count, face_count, 2, half_width, edge_cells)


def fold_edges(base, arrived_cols, arrived_rows, tile_rank, tile_count):
    half_width, row_count, edge_cells = (arrived_cols.shape[3], base.shape[2], base.shape[3])
    base = base.at[..., :half_width].add(
        jnp.swapaxes(arrived_cols[:, :, 0], -1, -2).astype(jnp.float32)
    )
    base = base.at[..., edge_cells - half_width :].add(
        jnp.swapaxes(arrived_cols[:, :, 1][:, :, ::-1, :], -1, -2).astype(jnp.float32)
    )
    top_add = jnp.where(tile_rank == 0, arrived_rows[:, :, 0].astype(jnp.float32), 0.0)
    base = base.at[:, :, :half_width].add(top_add)
    bottom_add = jnp.where(
        tile_rank == tile_count - 1, arrived_rows[:, :, 1][:, :, ::-1, :].astype(jnp.float32), 0.0
    )
    return base.at[:, :, row_count - half_width :].add(bottom_add)


def forward_rows(field, matrix, edge_peer, edge_flip, tile_rank, tile_count):
    half_width = (matrix.shape[1] - matrix.shape[0]) // 2
    row_count = field.shape[2]
    top_strip = field[:, :, :half_width]
    bottom_rows = field[:, :, row_count - half_width :]
    top_all, bottom_all = face_rows(top_strip, bottom_rows[:, :, ::-1])
    whole_cols = face_columns(column_strips(field, half_width))
    arrived = row_targets(edge_peer, edge_flip, top_all, bottom_all, whole_cols)
    beside_all = padded_2(
        jnp.concatenate([top_strip, bottom_rows], axis=2), (("tile", 2),), half_width
    )
    upper_rows = jnp.where(
        tile_rank == 0, arrived[:, :, 0][:, :, ::-1, :], beside_all[:, :, :half_width]
    )
    lower_rows = jnp.where(
        tile_rank == tile_count - 1, arrived[:, :, 1], beside_all[:, :, 3 * half_width :]
    )
    padded = jnp.concatenate([upper_rows, field, lower_rows], axis=2)
    return jnp.einsum("rc,mfcn->mfrn", matrix, padded, preferred_element_type=jnp.float32).astype(
        jnp.bfloat16
    )


def forward_cols(field, blocks, edge_peer, edge_flip, tile_rank):
    half_width = (blocks.shape[1] - blocks.shape[2]) // 2
    row_count = field.shape[2]
    top_all, bottom_all = face_rows(
        field[:, :, :half_width], field[:, :, row_count - half_width :][:, :, ::-1]
    )
    col_strips = column_strips(field, half_width)
    mirrored, whole_cols = spread_columns(col_strips, False)
    arrived = column_targets(
        edge_peer, edge_flip, tile_rank, top_all, bottom_all, col_strips, mirrored
    )
    left_side = jnp.swapaxes(arrived[:, :, 0][:, :, ::-1, :], -1, -2)
    right_side = jnp.swapaxes(arrived[:, :, 1], -1, -2)
    padded = jnp.concatenate([left_side, field, right_side], axis=3)
    return apply_cols(padded, blocks).astype(jnp.bfloat16)


def adjoint_cols(field, blocks, edge_peer, edge_flip, tile_rank, tile_count):
    half_width = (blocks.shape[1] - blocks.shape[2]) // 2
    member_count, face_count, row_count, edge_cells = field.shape
    spread = apply_cols_adjoint(field, blocks)
    interior = spread[..., half_width : half_width + edge_cells]
    left_rims = jnp.swapaxes(spread[..., :half_width][..., ::-1], -1, -2)
    right_rims = jnp.swapaxes(spread[..., edge_cells + half_width :], -1, -2)
    rims = jnp.stack([left_rims, right_rims], axis=2).astype(jnp.bfloat16)
    mirrored, whole_cols = spread_columns(rims, True)
    empty_rows = jnp.zeros((member_count, face_count, half_width, edge_cells), jnp.bfloat16)
    arrived_cols = column_targets(
        edge_peer, edge_flip, tile_rank, empty_rows, empty_rows, rims, mirrored
    )
    arrived_rows = row_targets(edge_peer, edge_flip, empty_rows, empty_rows, whole_cols)
    return fold_edges(interior, arrived_cols, arrived_rows, tile_rank, tile_count).astype(
        jnp.bfloat16
    )


def adjoint_rows(field, matrix, edge_peer, edge_flip, tile_rank, tile_count):
    half_width = (matrix.shape[1] - matrix.shape[0]) // 2
    member_count, face_count, row_count, edge_cells = field.shape
    spread = jnp.einsum("rc,mfrn->mfcn", matrix, field, preferred_element_type=jnp.float32)
    interior = spread[:, :, half_width : half_width + row_count]
    top_rims = spread[:, :, :half_width]
    bottom_rims = spread[:, :, row_count + half_width :]
    beside_all = padded_2(
        jnp.concatenate([top_rims, bottom_rims], axis=2).astype(jnp.bfloat16),
        (("tile", 2),),
        half_width,
    ).astype(jnp.float32)
    interior = interior.at[:, :, :half_width].add(beside_all[:, :, :half_width])
    interior = interior.at[:, :, row_count - half_width :].add(beside_all[:, :, 3 * half_width :])
    top_all, bottom_all = face_rows(
        top_rims[:, :, ::-1].astype(jnp.bfloat16), bottom_rims.astype(jnp.bfloat16)
    )
    empty_cols = jnp.zeros((member_count, face_count, 2, half_width, row_count), jnp.bfloat16)
    empty_whole = jnp.zeros((member_count, face_count, 2, half_width, edge_cells), jnp.bfloat16)
    arrived_cols = column_targets(
        edge_peer, edge_flip, tile_rank, top_all, bottom_all, empty_cols, empty_cols
    )
    arrived_rows = row_targets(edge_peer, edge_flip, top_all, bottom_all, empty_whole)
    return fold_edges(interior, arrived_cols, arrived_rows, tile_rank, tile_count)


def per_device(perturbations, control, band_rows, band_cols, edge_peer, edge_flip):
    half_width = band_cols.shape[1] // 2
    edge_cells = control.shape[-1]
    tile_rank = lax.axis_index("tile")
    tile_count = lax.axis_size("tile")
    matrix = row_matrix(filter_taps(band_rows, half_width), half_width)
    blocks = band_blocks(filter_taps(band_cols, half_width), min(128, edge_cells))
    member_wide = perturbations.astype(jnp.float32)
    weighted = (member_wide * control[None]).astype(jnp.bfloat16)
    section = forward_rows(weighted, matrix, edge_peer, edge_flip, tile_rank, tile_count)
    section = forward_cols(section, blocks, edge_peer, edge_flip, tile_rank)
    section = adjoint_cols(section, blocks, edge_peer, edge_flip, tile_rank, tile_count)
    filtered = adjoint_rows(section, matrix, edge_peer, edge_flip, tile_rank, tile_count)
    local_sum = jnp.sum(member_wide * filtered, axis=0)
    running = lax.psum(local_sum, "member")
    member_total = lax.axis_size("member") * perturbations.shape[0]
    return running / (member_total - 1.0)


def solution(mesh):
    return jax.shard_map(
        per_device,
        mesh=mesh,
        in_specs=(
            P("member", None, "tile", None),
            P(None, "tile", None),
            P("tile", None),
            P(),
            P(),
            P(),
        ),
        out_specs=P(None, "tile", None),
        check_vma=False,
    )
```

profile of v0, /device:TPU:1, one launch (start us, length us, event | category | flops | bytes accessed | tf_op | source)
XLA Modules:
  0.0 1254.8 jit_solution(15434243895905489467)
XLA Ops:
  9.1 4.7 collective-permute-start
  13.8 1.3 collective-permute-start.1
  16.0 4.6 rev.59
  20.6 1.3 select_bitcast_fusion
  26.7 120.3 %all_gather.6 = bf16[2,6,2,12,512]{3,4,1,0,2:T(8,128)(2,1)S(1)} all-gather(bf16[2,6,2,12,16]{3,4,1,0,2:T(8,128)(2,1)S(1)} %pad_maximum_fusion.11), channel_id=1, replica_groups=mesh['tile'=32,'member'=16] {'tile'}, dimensions={4}, use_global_device_ids=true | all-gather | bytes 304128 | tf_op jit(solution)/shard_map/all_gather | solution.py:93
  148.3 1.3 eq.75
  151.6 1.5 multiply_convert_fusion
  153.1 1.4 reshape.613
  154.5 1.6 copy.458
  156.0 2.6 fusion.4
  159.5 134.3 %all-reduce.17.cloned.1.call-done = (bf16[2,6,1,12,512]{3,4,1,0,2:T(8,128)(2,1)}, bf16[2,6,1,12,512]{4,3,1,0,2:T(8,128)(2,1)}) async-done(((bf16[2,6,1,12,512]{3,4,1,0,2:T(8,128)(2,1)}, bf16[2,6,1,12,512]{4,3,1,0,2:T(8,128)(2,1)}), (bf16[2,6,1,12,512]{3,4,1,0,2:T(8,128)(2,1)}, bf16[2,6,1,12,512]{4,3,1,0,2:T(8,128)(2,1)})) %all-reduce.17.cloned.1.call-update) | async-done | bytes 294928 | tf_op jit(solution)/shard_map/psum | solution.py:9
  293.8 2.4 copy.465
  296.3 5.5 pad_maximum_fusion
  301.8 5.4 copy.466
  308.7 3.0 rev.61
  315.5 1.9 collective-permute-start.2
  318.5 2.3 collective-permute-done.2
  320.9 1.9 collective-permute-start.3
  322.8 1.8 fusion.51
  324.6 24.0 %rev.64 = bf16[2,6,12,512]{2,3,1,0:T(8,128)(2,1)} reverse(bf16[2,6,12,512]{2,3,1,0:T(8,128)(2,1)} %get-tuple-element.188), dimensions={2} | reverse | bytes 294912 | tf_op jit(solution)/shard_map/rev | solution.py:186
  348.6 3.4 collective-permute-start.4
  352.1 1.3 broadcast_select_fusion
  355.2 6.1 collective-permute-start.5
  362.1 2.6 collective-permute-done.5
  364.7 11.9 collective-permute-start.6
  378.0 2.8 collective-permute-done.6
  380.9 253.4 %all-reduce.15.cloned.1.call-done = (bf16[2,6,12,512]{2,3,1,0:T(8,128)(2,1)}, bf16[2,6,12,512]{3,2,1,0:T(8,128)(2,1)}) async-done(((bf16[2,6,12,512]{2,3,1,0:T(8,128)(2,1)}, bf16[2,6,12,512]{3,2,1,0:T(8,128)(2,1)}), (bf16[2,6,12,512]{2,3,1,0:T(8,128)(2,1)}, bf16[2,6,12,512]{3,2,1,0:T(8,128)(2,1)})) %all-reduce.15.cloned.1.call-update) | async-done | bytes 294928 | tf_op jit(solution)/shard_map/psum | solution.py:9
  641.1 1.9 collective-permute-start.7
  643.8 3.2 collective-permute-done.7
  647.0 1.9 collective-permute-start.8
  649.0 76.3 %all_gather.7 = bf16[2,6,2,12,512]{3,2,1,0,4:T(2,128)(2,1)S(1)} all-gather(bf16[2,6,2,12,16]{3,2,1,0,4:T(2,128)(2,1)S(1)} %copy.498), channel_id=1, replica_groups=mesh['tile'=32,'member'=16] {'tile'}, dimensions={4}, use_global_device_ids=true | all-gather | bytes 304128 | tf_op jit(solution)/shard_map/all_gather | solution.py:93
  725.3 4.3 copy.550
  730.0 1.3 gather_fusion.5
  731.3 5.9 collective-permute-start.9
  737.5 3.0 rev.70
  741.5 2.3 collective-permute-start.10
  744.3 10.6 collective-permute-done.10
  754.8 9.4 collective-permute-start.11
  766.2 2.7 collective-permute-done.11
  771.6 2.0 scatter-add.55
  776.0 1.3 collective-permute-start.13
  777.3 4.0 collective-permute-start.12
  782.4 1.5 collective-permute-done.12
  784.9 279.8 %all-reduce.13.cloned.1.call-done = (bf16[2,6,12,512]{3,2,1,0:T(8,128)(2,1)}, bf16[2,6,12,512]{3,2,1,0:T(8,128)(2,1)}) async-done(((bf16[2,6,12,512]{3,2,1,0:T(8,128)(2,1)}, bf16[2,6,12,512]{3,2,1,0:T(8,128)(2,1)}), (bf16[2,6,12,512]{3,2,1,0:T(8,128)(2,1)}, bf16[2,6,12,512]{3,2,1,0:T(8,128)(2,1)})) %all-reduce.13.cloned.1.call-update) | async-done | bytes 294928 | tf_op jit(solution)/shard_map/psum | solution.py:9
  1070.9 3.0 rev.76
  1077.9 2.0 scatter-add.65
  1081.9 164.8 %all-reduce.11.cloned.1.call-done = f32[6,16,512]{2,1,0:T(8,128)} async-done(((f32[6,16,512]{2,1,0:T(8,128)}), f32[6,16,512]{2,1,0:T(8,128)}) %all-reduce.11.cloned.1.call-update) | async-done | bytes 196624 | tf_op jit(solution)/shard_map/psum | solution.py:258
  1246.7 1.6 broadcast_multiply_fusion
  (216 shorter events, 51.9 us)
Async XLA Ops:
  6.5 287.3 %all-reduce.17.cloned.1.call-start = ((), (), s32[]{:S(2)}) async-start(), calls=%async_computation.3 | async-start | bytes 3538944 | tf_op jit(solution)/shard_map/psum | solution.py:9
  9.1 303.6 %collective-permute-start = (bf16[2,6,12,512]{3,0,2,1:T(2,128)(2,1)}, bf16[2,6,12,512]{3,0,2,1:T(2,128)(2,1)}, u32[]{:S(2)}, u32[]{:S(2)}) collective-permute-start(bf16[2,6,12,512]{3,0,2,1:T(2,128)(2,1)} %copy.468), channel_id=1, source_target_pairs={{0,16},{16,32},{32,48},{48,64},{64,80},{80,96},{96,112},{112,128},... | collective-permute-start | bytes 442376 | tf_op jit(solution)/shard_map/ppermute | solution.py:23
  13.8 299.9 %collective-permute-start.1 = (bf16[2,6,12,512]{3,2,1,0:T(8,128)(2,1)S(1)}, bf16[2,6,12,512]{3,2,1,0:T(8,128)(2,1)}, u32[]{:S(2)}, u32[]{:S(2)}) collective-permute-start(bf16[2,6,12,512]{3,2,1,0:T(8,128)(2,1)S(1)} %get-tuple-element.211), channel_id=1, source_target_pairs={{16,0},{32,16},{48,32},{64,48},{80,64},{96,80},{112,96},{128,112},... | collective-permute-start | bytes 442376 | tf_op jit(solution)/shard_map/ppermute | solution.py:24
  21.9 2.1 copy-start.16
  21.9 612.4 %all-reduce.15.cloned.1.call-start = ((), (), s32[]{:S(2)}) async-start(), calls=%async_computation.2 | async-start | bytes 3538944 | tf_op jit(solution)/shard_map/psum | solution.py:9
  26.7 120.3 %copy-start.15 = (s32[6,4]{0,1:T(4,128)S(1)}, s32[6,4]{0,1:T(4,128)}, u32[]{:S(2)}) copy-start(s32[6,4]{0,1:T(4,128)} %param.43) | copy-start | bytes 292
  26.7 124.2 %copy-start.7 = (f32[16,25]{1,0:T(8,128)S(1)}, f32[16,25]{1,0:T(8,128)}, u32[]{:S(2)}) copy-start(f32[16,25]{1,0:T(8,128)} %param.40) | copy-start | bytes 4804
  156.0 3.2 copy-start.8
  156.0 3.2 copy-start.14
  159.2 148.0 %copy-start.9 = (s32[1024]{0:T(1024)}, s32[1024]{0:T(1024)S(1)}, u32[]{:S(2)}) copy-start(s32[1024]{0:T(1024)S(1)} %pad_clamp_fusion.1) | copy-start | bytes 12292
  307.2 4.5 copy-start.10
  313.7 3.7 copy-start.18
  313.7 3.7 copy-start.19
  313.7 3.9 copy-start.3
  315.5 5.4 collective-permute-start.2
  317.7 320.9 %copy-start.12 = (pred[12]{0:T(512)(128)(4,1)}, pred[12]{0:T(512)(128)(4,1)S(1)}, u32[]{:S(2)}) copy-start(pred[12]{0:T(512)(128)(4,1)S(1)} %eq.72) | copy-start | bytes 40
  320.9 27.7 %collective-permute-start.3 = (bf16[2,6,2,12,16]{4,3,1,0,2:T(8,128)(2,1)S(1)}, bf16[2,6,2,12,16]{4,3,1,0,2:T(8,128)(2,1)}, u32[]{:S(2)}, u32[]{:S(2)}) collective-permute-start(bf16[2,6,2,12,16]{4,3,1,0,2:T(8,128)(2,1)S(1)} %collective-permute-done.2), channel_id=1, source_target_pairs={{0,32},{16,48},{32,0},{48,16},{64,96},{80,112},{96,64},{112,80},{1... | collective-permute-start | bytes 27656 | tf_op jit(solution)/shard_map/ppermute | solution.py:13
  348.6 6.6 collective-permute-start.4
  355.2 9.5 collective-permute-start.5
  362.0 702.6 %all-reduce.13.cloned.1.call-start = ((), (), s32[]{:S(2)}) async-start(), calls=%async_computation.1 | async-start | bytes 786432 | tf_op jit(solution)/shard_map/psum | solution.py:9
  364.7 16.1 %collective-permute-start.6 = (bf16[2,6,2,12,16]{4,3,1,0,2:T(8,128)(2,1)S(1)}, bf16[2,6,2,12,16]{4,3,1,0,2:T(8,128)(2,1)S(1)}, u32[]{:S(2)}, u32[]{:S(2)}) collective-permute-start(bf16[2,6,2,12,16]{4,3,1,0,2:T(8,128)(2,1)S(1)} %collective-permute-done.5), channel_id=1, source_target_pairs={{0,256},{16,272},{32,288},{48,304},{64,320},{80,336},{96,352},{112... | collective-permute-start | bytes 27656 | tf_op jit(solution)/shard_map/ppermute | solution.py:13
  635.1 3.5 copy-start.5
  636.4 2.9 copy-start.4
  640.9 6.2 copy-start
  641.1 5.9 collective-permute-start.7
  647.0 84.2 %collective-permute-start.8 = (bf16[2,6,2,12,16]{3,4,1,0,2:T(8,128)(2,1)}, bf16[2,6,2,12,16]{3,4,1,0,2:T(8,128)(2,1)}, u32[]{:S(2)}, u32[]{:S(2)}) collective-permute-start(bf16[2,6,2,12,16]{3,4,1,0,2:T(8,128)(2,1)} %collective-permute-done.7), channel_id=1, source_target_pairs={{0,32},{16,48},{32,0},{48,16},{64,96},{80,112},{96,64},{112,80},{1... | collective-permute-start | bytes 27656 | tf_op jit(solution)/shard_map/ppermute | solution.py:13
  729.6 14.2 %copy-start.11 = (pred[12]{0:T(512)(128)(4,1)S(1)}, pred[12]{0:T(512)(128)(4,1)}, u32[]{:S(2)}) copy-start(pred[12]{0:T(512)(128)(4,1)} %eq.75) | copy-start | bytes 40
  731.2 33.4 %copy-start.1 = (f32[2,6,16,536]{3,2,1,0:T(8,128)S(1)}, f32[2,6,16,536]{3,2,1,0:T(8,128)}, u32[]{:S(2)}) copy-start(f32[2,6,16,536]{3,2,1,0:T(8,128)} %copy-done) | copy-start | bytes 1234948
  731.3 10.3 collective-permute-start.9
  741.5 13.3 %collective-permute-start.10 = (bf16[2,6,2,12,16]{3,4,1,0,2:T(8,128)(2,1)S(1)}, bf16[2,6,2,12,16]{3,4,1,0,2:T(8,128)(2,1)S(1)}, u32[]{:S(2)}, u32[]{:S(2)}) collective-permute-start(bf16[2,6,2,12,16]{3,4,1,0,2:T(8,128)(2,1)S(1)} %collective-permute-done.9), channel_id=1, source_target_pairs={{0,128},{16,144},{32,160},{48,176},{64,192},{80,208},{96,224},{112... | collective-permute-start | bytes 27656 | tf_op jit(solution)/shard_map/ppermute | solution.py:13
  754.8 14.1 %collective-permute-start.11 = (bf16[2,6,2,12,16]{3,4,1,0,2:T(8,128)(2,1)S(1)}, bf16[2,6,2,12,16]{3,4,1,0,2:T(8,128)(2,1)S(1)}, u32[]{:S(2)}, u32[]{:S(2)}) collective-permute-start(bf16[2,6,2,12,16]{3,4,1,0,2:T(8,128)(2,1)S(1)} %collective-permute-done.10), channel_id=1, source_target_pairs={{0,256},{16,272},{32,288},{48,304},{64,320},{80,336},{96,352},{112... | collective-permute-start | bytes 27656 | tf_op jit(solution)/shard_map/ppermute | solution.py:13
  764.7 5.7 copy-start.6
  764.7 5.7 copy-start.13
  776.0 6.3 collective-permute-start.13
  777.3 6.6 collective-permute-start.12
  782.1 464.6 %all-reduce.11.cloned.1.call-start = ((), (), s32[]{:S(2)}) async-start(), calls=%async_computation | async-start | bytes 393216 | tf_op jit(solution)/shard_map/psum | solution.py:258
  784.4 284.3 %copy-start.17 = (bf16[4]{0:T(256)(128)(2,1)S(1)}, bf16[4]{0:T(256)(128)(2,1)}, u32[]{:S(2)}) copy-start(bf16[4]{0:T(256)(128)(2,1)} %pad.33.clone) | copy-start | bytes 28
  1079.9 1.2 copy-start.2
Sparse Core Ops, SparseCore 0:
  22.0 271.7 all-reduce.16
  362.2 272.0 all-reduce.14
  782.2 282.4 all-reduce.12
  1082.0 164.6 all-reduce.10
where the time goes:
time: 1260 us; the launch traced here: 1250 us
  waiting for transfers between devices  860 us (68%)
  blocking collectives  197 us (16%)
  local copies, waits for them, and re-layouts  90.7 us (7%)
  starting transfers between devices  58.3 us (5%)
  other arithmetic  29.1 us (2%)
  between operations  15.7 us (1%)
    psum x3, waiting for transfers between devices, spread_2(): return lax.psum(kept, axis)  667 us
    all_gather x2, blocking collectives, face_columns(): return lax.all_gather(col_strips, 'tile', axis=4, tiled=True)  197 us
    psum x1, waiting for transfers between devices, per_device(): running = lax.psum(local_sum, 'member')  165 us
    ppermute x10, starting transfers between devices, from_partner(): lax.ppermute(value, axis, [(i, i ^ 1 << distance) for i in range(lax.axis...  46.7 us
    ppermute x10, waiting for transfers between devices, from_partner(): lax.ppermute(value, axis, [(i, i ^ 1 << distance) for i in range(lax.axis...  26.4 us
  transfers between devices with their start and end apart: 18, of which 13 were waited for; matrix products, arithmetic and copies ran while one was open for 7% of the time, Pallas kernels for 0%

commit v1 on v0

v1 whole, which is shorter than its diff:
```python
import functools
import math

import jax
import jax.numpy as jnp
import numpy as np
from jax import lax
from jax.experimental import pallas as pl
from jax.experimental.pallas import tpu as pltpu
from jax.sharding import PartitionSpec as P

HALF = 12
ROWS = 16
FACES = 6
LANES = 128
FR = FACES * ROWS
COLW = 256
FLIPPED = 24 << 4
f32, bf16, i32 = jnp.float32, jnp.bfloat16, jnp.int32


def iota(shape, dim):
    return lax.broadcasted_iota(i32, shape, dim)


def dot(a, b):
    return lax.dot_general(a, b, (((1,), (0,)), ((), ())), preferred_element_type=f32)


def dot_nt(a, b):
    return lax.dot_general(a, b, (((1,), (1,)), ((), ())), preferred_element_type=f32)


def dot_tn(a, b):
    return lax.dot_general(a, b, (((0,), (0,)), ((), ())), preferred_element_type=f32)


def onehot(mask):
    return jnp.where(mask, 1.0, 0.0).astype(bf16)


def taper(band):
    rows, taps = band.shape
    steps = np.arange(2 * HALF + 1, dtype=np.float32) - HALF
    curve = np.exp(-((steps / HALF) ** 2))
    scale = 1.0 / math.sqrt(math.sqrt(float(np.sum(curve * curve))) * float(np.sum(curve)))
    lane = iota((1, taps), 1).astype(f32)
    g = jnp.exp(-(((lane - HALF) / HALF) ** 2)) * scale
    wide = jnp.concatenate([band * g, jnp.zeros((rows, LANES - taps), f32)], axis=1)
    return wide.astype(bf16).astype(f32)


def col_key(lane):
    face, rest = lane >> 5, lane & 31
    second = rest >= HALF
    layer = jnp.where(second, rest - HALF, rest)
    edge = jnp.where(second, 3, 2)
    good = (rest < 2 * HALF) & (face < FACES)
    return jnp.where(good, ((4 * face + edge) << 4) + layer, -1)


def row_key(index, edge, backwards):
    face, rest = index >> 4, index & 15
    layer = ROWS - 1 - rest if backwards else rest
    good = (layer < HALF) & (face < FACES)
    return jnp.where(good, ((4 * face + edge) << 4) + layer, -1)


def wanted_cols(lane, peer, flip):
    face, rest = lane >> 5, lane & 31
    second = rest >= HALF
    layer = jnp.where(second, rest - HALF, rest)
    good = (rest < 2 * HALF) & (face < FACES)
    base = jnp.zeros(lane.shape, i32)
    for f in range(FACES):
        for e in (2, 3):
            here = (face == f) & (second == (e == 3))
            base = jnp.where(here, (peer[f, e] << 4) + flip[f, e] * FLIPPED, base)
    return jnp.where(good, base + layer, -2)


def wanted_rows(index, peer, flip, hub, backwards):
    turned = index >= FR
    within = jnp.where(turned, index - FR, index)
    face, rest = within >> 4, within & 15
    layer = jnp.where(backwards, ROWS - 1 - rest, rest)
    base = jnp.zeros(index.shape, i32)
    here_turned = jnp.zeros(index.shape, i32)
    for f in range(FACES):
        base = jnp.where(face == f, peer[f, hub] << 4, base)
        here_turned = jnp.where(face == f, flip[f, hub], here_turned)
    good = (layer < HALF) & ((here_turned == 1) == turned)
    return jnp.where(good, base + layer, -2)


def tile_kernel(
    tiles, members,
    pert, control, band_rows, band_cols, peer, flip, out,
    wp, pa, pall_a, pb, pb_mir, qb, qr_b, pc, pc_mir, pall_c, ds, drs, qd, qr_d,
    dmat, xs, zacc, bd, bdt, jn, gmat,
    ring_s, ring_r, hub_s, hub_r, mir_s, mir_r, sc_s, sc_r,
):
    T, M = tiles, members
    N = ROWS * T
    NB = N // LANES
    t = lax.axis_index("tile")
    prev, nxt, mirror = lax.rem(t + T - 1, T), lax.rem(t + 1, T), T - 1 - t
    hub = jnp.where(t == T - 1, 1, 0)
    is_hub = (t == 0) | (t == T - 1)
    last = hub == 1

    def remote(src, dst, send, recv, where):
        return pltpu.make_async_remote_copy(
            src_ref=src, dst_ref=dst, send_sem=send, recv_sem=recv,
            device_id={"tile": where}, device_id_type=pl.DeviceIdType.MESH,
        )

    barrier = pltpu.get_barrier_semaphore()

    def greet(where):
        pl.semaphore_signal(
            barrier, inc=1, device_id={"tile": where}, device_id_type=pl.DeviceIdType.MESH
        )

    for where in (prev, nxt, mirror):
        greet(where)

    @pl.when(is_hub)
    def _():
        def body(i, carry):
            greet(lax.rem(t + i, T))
            return carry

        lax.fori_loop(1, T, body, 0)

    @pl.when(jnp.logical_not(is_hub))
    def _():
        greet(0)
        greet(T - 1)

    r256, c128 = iota((2 * LANES, LANES), 0), iota((2 * LANES, LANES), 1) & 31
    sel = onehot(
        ((r256 < HALF) & (c128 == r256))
        | ((r256 >= 2 * LANES - HALF) & (c128 == HALF + 2 * LANES - 1 - r256))
    )
    group = iota((ROWS, LANES), 1) >> 5

    def pack(quad):
        packs = []
        for m in range(M):
            blocks = []
            for g in range(2):
                block = jnp.zeros((ROWS, LANES), f32)
                for q in range(4):
                    f = 4 * g + q
                    if f < FACES:
                        at = (m * FACES + f) * ROWS
                        block = jnp.where(group == q, quad[at : at + ROWS], block)
                blocks.append(block)
            packs.append(jnp.concatenate(blocks, axis=1).astype(bf16))
        return packs

    def pack_ends(flat):
        ends = jnp.concatenate([flat[:, :LANES], flat[:, N - LANES :]], axis=1)
        return pack(dot(ends, sel))

    def spread(packs):
        parts = []
        for m in range(M):
            for f in range(FACES):
                g, q = f // 4, f % 4
                block = packs[m][:, g * LANES : (g + 1) * LANES]
                parts.append(jnp.where(group == q, block, 0.0))
        return jnp.concatenate(parts, axis=0).astype(bf16)

    for m in range(M):
        wp[1, m] = (pert[m].astype(f32) * control[...]).astype(bf16)
    own = wp[1].reshape(M * FR, N)
    for m, value in enumerate(pack_ends(own)):
        pa[m] = value

    @pl.when(is_hub)
    def _():
        pl.semaphore_wait(barrier, 3 + T - 1)

    @pl.when(jnp.logical_not(is_hub))
    def _():
        pl.semaphore_wait(barrier, 5)

    ring_a = [
        remote(wp.at[1], wp.at[2], ring_s.at[0], ring_r.at[0], prev),
        remote(wp.at[1], wp.at[0], ring_s.at[1], ring_r.at[1], nxt),
    ]
    for copy in ring_a:
        copy.start()

    def hub_copies(src, dst, base):
        return [
            remote(src, dst.at[:, t], hub_s.at[base + h], hub_r.at[base // 2], h * (T - 1))
            for h in range(2)
        ]

    def start_to_hubs(copies):
        for h in range(2):
            @pl.when(t != h * (T - 1))
            def _():
                copies[h].start()

    def finish_to_hubs(copies):
        for h in range(2):
            @pl.when(t != h * (T - 1))
            def _():
                copies[h].wait_send()

    def wait_at_hub(dst, base):
        others = dst.at[:, pl.ds(0, T - 1)]
        pltpu.make_async_copy(others, others, hub_r.at[base // 2]).wait()

    to_hubs_a = hub_copies(pa, pall_a, 0)
    start_to_hubs(to_hubs_a)

    lane = iota((LANES, LANES), 1)
    blocks = {}
    for b in range(NB):
        wide = taper(band_cols[b * LANES : (b + 1) * LANES, :])
        wide = jnp.concatenate([wide, jnp.zeros((LANES, LANES), f32)], axis=1)
        wide = pltpu.roll(wide, 0, 1, stride=1, stride_axis=0)
        wide = pltpu.roll(wide, 2 * LANES - HALF, 1)
        over = wide[:, LANES:]
        for c, value in (
            (b, wide[:, :LANES]),
            ((b + 1) % (NB + 1), jnp.where(lane < HALF, over, 0.0)),
            ((b + NB) % (NB + 1), jnp.where(lane >= LANES - HALF, over, 0.0)),
        ):
            blocks[b, c] = blocks[b, c] + value if (b, c) in blocks else value
    from_lane, to_lane = iota((LANES, LANES), 0), iota((LANES, LANES), 1) & 31
    rim_order = onehot(
        ((to_lane < HALF) & (from_lane == LANES - 1 - to_lane))
        | ((to_lane >= HALF) & (to_lane < 2 * HALF) & (from_lane == to_lane - HALF))
    )
    for b in range(NB):
        for c in range(NB + 1):
            value = blocks.get((b, c))
            value = jnp.zeros((LANES, LANES), bf16) if value is None else value.astype(bf16)
            if c == NB:
                value = dot(value, rim_order).astype(bf16)
            dmat[b * LANES : (b + 1) * LANES, c * LANES : (c + 1) * LANES] = value

    taps = taper(band_rows[...])
    base = jnp.concatenate([taps, jnp.zeros((ROWS, LANES), f32)], axis=1)
    skew = pltpu.roll(base, ROWS - HALF, 1, stride=1, stride_axis=0)
    skew = skew[:, :LANES].astype(bf16)
    six = jnp.concatenate([skew] * FACES, axis=0)
    e0, e1 = iota((LANES, 3 * LANES), 0), iota((LANES, 3 * LANES), 1)
    expand = onehot((e0 == ((e1 >> 7) << 4) + (e1 & 15)) & ((e1 & 127) < FR))
    k0, k1 = iota((FR, 3 * LANES), 0), iota((FR, 3 * LANES), 1)
    band = jnp.where((k0 >> 4) == ((k1 & 127) >> 4), dot(six, expand), 0.0)
    for p in range(3):
        part = band[:, p * LANES : (p + 1) * LANES]
        bd[p] = part[:, :FR].astype(bf16)
        square = jnp.concatenate([part, jnp.zeros((LANES - FR, LANES), f32)], axis=0)
        bdt[p] = jnp.transpose(square)[:FR, :FR].astype(bf16)

    want = wanted_cols(iota((COLW, COLW), 1), peer, flip)
    src = iota((COLW, COLW), 0)
    from_cols = col_key(src)
    upper = src < LANES
    from_rows = row_key(jnp.where(upper, src, src - LANES), jnp.where(upper, 0, 1), False)
    turn = jnp.where(want >= FLIPPED, want - FLIPPED, want)
    straight = want < FLIPPED
    is_cols, is_rows = from_cols == turn, from_rows == turn
    gmat[0] = onehot(is_cols & straight)
    gmat[1] = onehot(is_rows & straight)
    gmat[2] = onehot(is_cols & jnp.logical_not(straight))
    gmat[3] = onehot(is_rows & jnp.logical_not(straight))
    back = onehot(iota((ROWS, ROWS), 0) + iota((ROWS, ROWS), 1) == ROWS - 1)

    @pl.when(is_hub)
    def _():
        jn[...] = onehot(iota((N, N), 0) + iota((N, N), 1) == N - 1)

    def gather_rows(cols, rows, store, dst_back, src_back):
        want_r = wanted_rows(iota((2 * FR, COLW), 0), peer, flip, hub, dst_back)
        s_cols = onehot(want_r == col_key(iota((2 * FR, COLW), 1)))
        if rows is not None:
            want_e = wanted_rows(iota((2 * FR, FR), 0), peer, flip, hub, dst_back)
            s_rows = [
                onehot(want_e == row_key(iota((2 * FR, FR), 1), h, src_back[h]))
                for h in range(2)
            ]
        for m in range(M):
            total = jnp.zeros((2 * FR, N), f32)
            if cols is not None:
                total = total + dot_nt(s_cols, cols[m].reshape(N, COLW))
            if rows is not None:
                total = total + dot(s_rows[0], rows[1 + hub, m].reshape(FR, N))
                total = total + dot(s_rows[1], rows[hub, m].reshape(FR, N))
            store(m, total[:FR] + dot(total[FR:].astype(bf16), jn[...]))

    def scatter(flat, q, qr, base, back_of_first):
        s0, s1 = iota((FR, LANES), 0), iota((FR, LANES), 1)
        row = s0 & 15
        layer = jnp.where(last != back_of_first, ROWS - 1 - row, row)
        pick = onehot((layer < HALF) & (s1 == ((s0 >> 4) << 4) + layer))
        for m in range(M):
            q[m] = dot_tn(flat(m), pick).astype(bf16).reshape(T, ROWS, LANES)

        def body(i, carry):
            there = lax.rem(t + i, T)
            for turned, block in ((0, there), (1, T - 1 - there)):
                remote(
                    q.at[:, block], qr.at[hub, turned],
                    sc_s.at[base, turned], sc_r.at[base, hub, turned], there,
                ).start()
            return carry

        lax.fori_loop(1, T, body, 0)
        qr[hub, 0] = q[:, t]
        qr[hub, 1] = q[:, mirror]

    def finish_scatter(q, base):
        others = q.at[:, pl.ds(0, T - 1)]
        for turned in range(2):
            pltpu.make_async_copy(others, others, sc_s.at[base, turned]).wait()

    def wait_scatter(q, qr, base):
        for h in range(2):
            @pl.when(t != h * (T - 1))
            def _():
                for turned in range(2):
                    remote(
                        q.at[:, 0], qr.at[h, turned],
                        sc_s.at[base, turned], sc_r.at[base, h, turned], h * (T - 1),
                    ).wait_recv()

    def arrive_cols(direct, mirrored, qr):
        packs = []
        for m in range(M):
            straight, turned = jnp.zeros((ROWS, COLW), f32), jnp.zeros((ROWS, COLW), f32)
            if direct is not None:
                straight = straight + dot(direct[m], gmat[0])
                turned = turned + dot(mirrored[m], gmat[2])
            if qr is not None:
                near = jnp.concatenate([qr[0, 0, m], qr[1, 0, m]], axis=1)
                far = jnp.concatenate([qr[0, 1, m], qr[1, 1, m]], axis=1)
                straight = straight + dot(near, gmat[1])
                turned = turned + dot(far, gmat[3])
            packs.append(straight + dot(back, turned.astype(bf16)))
        return packs

    for copy in ring_a:
        copy.wait_recv()

    @pl.when(is_hub)
    def _():
        pall_a[:, t] = pa[...]
        wait_at_hub(pall_a, 0)
        got = [None] * M

        def keep(m, value):
            got[m] = value.astype(bf16).reshape(FACES, ROWS, N)

        gather_rows(pall_a, wp, keep, jnp.logical_not(last), (False, True))
        for m in range(M):
            wp[2 * hub, m] = got[m]

    for m in range(M):
        x = dot(bd[0], wp[0, m].reshape(FR, N))
        x = x + dot(bd[1], wp[1, m].reshape(FR, N))
        x = x + dot(bd[2], wp[2, m].reshape(FR, N))
        xs[m * FR : (m + 1) * FR, :N] = x.astype(bf16)

    @pl.when(is_hub)
    def _():
        scatter(lambda m: xs[m * FR : (m + 1) * FR, :N], qb, qr_b, 0, False)

    for m, value in enumerate(pack_ends(xs[:, :N])):
        pb[m] = value
    mirror_b = remote(pb, pb_mir, mir_s.at[0], mir_r.at[0], mirror)
    mirror_b.start()
    mirror_b.wait_recv()
    wait_scatter(qb, qr_b, 0)
    xs[:, N:] = spread(arrive_cols(pb, pb_mir, qr_b))
    y = dot_nt(xs[...], dmat[...]).astype(bf16)

    zrim = dot(y, dmat[:, N:])
    for m, value in enumerate(pack(zrim)):
        pc[m] = value
    mirror_c = remote(pc, pc_mir, mir_s.at[1], mir_r.at[1], mirror)
    mirror_c.start()
    to_hubs_c = hub_copies(pc, pall_c, 2)
    start_to_hubs(to_hubs_c)
    zacc[...] = dot(y, dmat[:, :N])
    mirror_c.wait_recv()

    @pl.when(is_hub)
    def _():
        pall_c[:, t] = pc[...]
        wait_at_hub(pall_c, 2)

        def add(m, value):
            zacc[m * FR : (m + 1) * FR, :] += value

        gather_rows(pall_c, None, add, last, None)

    ends = dot_nt(spread(arrive_cols(pc, pc_mir, None)), sel)
    zacc[:, :LANES] += ends[:, :LANES]
    zacc[:, N - LANES :] += ends[:, LANES:]

    ring_d = [
        remote(ds.at[0], drs.at[2], ring_s.at[2], ring_r.at[2], prev),
        remote(ds.at[1], drs.at[0], ring_s.at[3], ring_r.at[3], nxt),
    ]
    for m in range(M):
        z = zacc[m * FR : (m + 1) * FR, :].astype(bf16)
        ds[0, m] = dot(bdt[0], z).astype(bf16).reshape(FACES, ROWS, N)
        ds[1, m] = dot(bdt[2], z).astype(bf16).reshape(FACES, ROWS, N)
        zacc[m * FR : (m + 1) * FR, :] = dot(bdt[1], z)
    for copy in ring_d:
        copy.start()

    @pl.when(is_hub)
    def _():
        scatter(lambda m: ds[hub, m].reshape(FR, N), qd, qr_d, 1, True)
        drs[1] = ds[hub]

    for copy in ring_d:
        copy.wait_recv()

    @pl.when(is_hub)
    def _():
        got = [None] * M

        def keep(m, value):
            got[m] = value.astype(bf16).reshape(FACES, ROWS, N)

        gather_rows(None, drs, keep, last, (True, False))
        for m in range(M):
            drs[2 * hub, m] = got[m]

    wait_scatter(qd, qr_d, 1)
    ends = dot_nt(spread(arrive_cols(None, None, qr_d)), sel)
    zacc[:, :LANES] += ends[:, :LANES]
    zacc[:, N - LANES :] += ends[:, LANES:]

    total = jnp.zeros((FR, N), f32)
    for m in range(M):
        spill = drs[0, m].astype(f32) + drs[2, m].astype(f32)
        filtered = zacc[m * FR : (m + 1) * FR, :] + spill.reshape(FR, N)
        total = total + pert[m].astype(f32).reshape(FR, N) * filtered
    chunks, per_chunk = out.shape[:2]
    for u in range(chunks * per_chunk):
        r, c = u // NB, u % NB
        out[u // per_chunk, u % per_chunk] = total[r * 8 : r * 8 + 8, c * LANES : (c + 1) * LANES]

    for copy in ring_a + ring_d + [mirror_b, mirror_c]:
        copy.wait_send()
    finish_to_hubs(to_hubs_a)
    finish_to_hubs(to_hubs_c)

    @pl.when(is_hub)
    def _():
        finish_scatter(qb, 0)
        finish_scatter(qd, 1)


def member_kernel(count, ensemble, part, out, got, mine, done, s1, r1, s2, r2):
    me = lax.axis_index("member")

    def remote(src, dst, send, recv, where):
        return pltpu.make_async_remote_copy(
            src_ref=src, dst_ref=dst, send_sem=send, recv_sem=recv,
            device_id={"member": where}, device_id_type=pl.DeviceIdType.MESH,
        )

    barrier = pltpu.get_barrier_semaphore()
    for i in range(1, count):
        pl.semaphore_signal(
            barrier, inc=1, device_id={"member": lax.rem(me + i, count)},
            device_id_type=pl.DeviceIdType.MESH,
        )
    pl.semaphore_wait(barrier, count - 1)
    for i in range(1, count):
        there = lax.rem(me + i, count)
        remote(part.at[there], got.at[me], s1, r1, there).start()
    got[me] = part[me]
    others = got.at[pl.ds(0, count - 1)]
    pltpu.make_async_copy(others, others, r1).wait()
    total = got[0]
    for i in range(1, count):
        total = total + got[i]
    mine[...] = total
    for i in range(1, count):
        there = lax.rem(me + i, count)
        remote(mine, done.at[me], s2, r2, there).start()
    done[me] = total
    others = done.at[pl.ds(0, count - 1)]
    pltpu.make_async_copy(others, others, r2).wait()
    per_chunk = part.shape[1]
    blocks = out.shape[1] // LANES
    scale = 1.0 / (ensemble - 1.0)
    for u in range(count * per_chunk):
        r, c = u // blocks, u % blocks
        out[r * 8 : r * 8 + 8, c * LANES : (c + 1) * LANES] = (
            done[u // per_chunk, u % per_chunk] * scale
        )
    others = got.at[pl.ds(0, count - 1)]
    pltpu.make_async_copy(others, others, s1).wait()
    pltpu.make_async_copy(others, others, s2).wait()


def per_device(perturbations, control, band_rows, band_cols, edge_peer, edge_flip):
    T, count = lax.axis_size("tile"), lax.axis_size("member")
    M = perturbations.shape[0]
    N = control.shape[-1]
    units = FR * N // (8 * LANES)
    per_chunk = units // count
    vmem, smem = pl.BlockSpec(memory_space=pltpu.VMEM), pl.BlockSpec(memory_space=pltpu.SMEM)
    dma = pltpu.SemaphoreType.DMA
    part = pl.pallas_call(
        functools.partial(tile_kernel, T, M),
        out_shape=jax.ShapeDtypeStruct((count, per_chunk, 8, LANES), f32),
        in_specs=[vmem, vmem, vmem, vmem, smem, smem],
        out_specs=vmem,
        scratch_shapes=[
            pltpu.VMEM((3, M, FACES, ROWS, N), bf16),
            pltpu.VMEM((M, ROWS, COLW), bf16),
            pltpu.VMEM((M, T, ROWS, COLW), bf16),
            pltpu.VMEM((M, ROWS, COLW), bf16),
            pltpu.VMEM((M, ROWS, COLW), bf16),
            pltpu.VMEM((M, T, ROWS, LANES), bf16),
            pltpu.VMEM((2, 2, M, ROWS, LANES), bf16),
            pltpu.VMEM((M, ROWS, COLW), bf16),
            pltpu.VMEM((M, ROWS, COLW), bf16),
            pltpu.VMEM((M, T, ROWS, COLW), bf16),
            pltpu.VMEM((2, M, FACES, ROWS, N), bf16),
            pltpu.VMEM((3, M, FACES, ROWS, N), bf16),
            pltpu.VMEM((M, T, ROWS, LANES), bf16),
            pltpu.VMEM((2, 2, M, ROWS, LANES), bf16),
            pltpu.VMEM((N, N + LANES), bf16),
            pltpu.VMEM((M * FR, N + LANES), bf16),
            pltpu.VMEM((M * FR, N), f32),
            pltpu.VMEM((3, FR, FR), bf16),
            pltpu.VMEM((3, FR, FR), bf16),
            pltpu.VMEM((N, N), bf16),
            pltpu.VMEM((4, COLW, COLW), bf16),
            dma((4,)), dma((4,)),
            dma((4,)), dma((2,)),
            dma((2,)), dma((2,)),
            dma((2, 2)), dma((2, 2, 2)),
        ],
        compiler_params=pltpu.CompilerParams(
            collective_id=0, has_side_effects=True, vmem_limit_bytes=40 * 1024 * 1024
        ),
        name="filters",
    )(perturbations, control, band_rows, band_cols, edge_peer, edge_flip)
    whole = pl.pallas_call(
        functools.partial(member_kernel, count, count * M),
        out_shape=jax.ShapeDtypeStruct((FR, N), f32),
        in_specs=[vmem],
        out_specs=vmem,
        scratch_shapes=[
            pltpu.VMEM((count, per_chunk, 8, LANES), f32),
            pltpu.VMEM((per_chunk, 8, LANES), f32),
            pltpu.VMEM((count, per_chunk, 8, LANES), f32),
            dma, dma, dma, dma,
        ],
        compiler_params=pltpu.CompilerParams(
            collective_id=1, has_side_effects=True, vmem_limit_bytes=8 * 1024 * 1024
        ),
        name="member_sum",
    )(part)
    return whole.reshape(control.shape)


def solution(mesh):
    return jax.shard_map(
        per_device,
        mesh=mesh,
        in_specs=(
            P("member", None, "tile", None),
            P(None, "tile", None),
            P("tile", None),
            P(),
            P(),
            P(),
        ),
        out_specs=P(None, "tile", None),
        check_vma=False,
    )
```

time: 1260 us -> 78.2 us (0.06)
  waiting for transfers between devices: 860 us -> 0 us
  blocking collectives: 197 us -> 0 us
  local copies, waits for them, and re-layouts: 90.7 us -> 3.5 us
  Pallas kernels: 0 us -> 74.4 us
  starting transfers between devices: 58.3 us -> 0 us
  other arithmetic: 29.1 us -> 0 us
  between operations: 15.7 us -> 0.05 us
    psum x4 -> x0, waiting for transfers between devices: 832 us -> none  [the longest x3 667 us: spread_2(): return lax.psum(kept, axis)]
    all_gather x2 -> x0, blocking collectives: 197 us -> none  [face_columns(): return lax.all_gather(col_strips, 'tile', axis=4, tiled=True)]
    pallas_call x0 -> x2, Pallas kernels: none -> 74.4 us  [the longest x1 52.2 us: per_device(): pl.pallas_call(functools.partial(tile_kernel, T, M), out_shape=jax.ShapeD...]
    ppermute x14 -> x0, starting transfers between devices: 57.9 us -> none  [the longest x10 46.7 us: from_partner(): lax.ppermute(value, axis, [(i, i ^ 1 << distance) for i in range(lax.axis...]
    rev x18 -> x0, local copies, waits for them, and re-layouts: 39.6 us -> none  [the longest x1 24 us: forward_cols(): field[:, :, row_count - half_width:][:, :, ::-1]]
    ppermute x14 -> x0, waiting for transfers between devices: 27.9 us -> none  [the longest x10 26.4 us: from_partner(): lax.ppermute(value, axis, [(i, i ^ 1 << distance) for i in range(lax.axis...]
    another operation x27 -> x0, local copies, waits for them, and re-layouts: 14.1 us -> none  [the longest x5 8.63 us: row_targets(): jnp.stack([top_all, bottom_all, whole_cols[:, :, 0], whole_cols[:, :, 1]]...]
  transfers between devices with their start and end apart: 18 -> 0, of which waited for: 13 -> 0; matrix products, arithmetic and copies ran while one was open for 7% -> 0% of each run, Pallas kernels for 0% -> 0%
where the time goes in v1:
time: 78.2 us; the launch traced here: 78 us
  Pallas kernels  74.4 us (95%)
  local copies, waits for them, and re-layouts  3.5 us (4%)
    pallas_call x1, Pallas kernels, per_device(): pl.pallas_call(functools.partial(tile_kernel, T, M), out_shape=jax.ShapeD...  52.2 us
    pallas_call x1, Pallas kernels, per_device(): pl.pallas_call(functools.partial(member_kernel, count, count * M), out_sh...  22.2 us
    unnamed x12, local copies, waits for them, and re-layouts  3.5 us

profile of v1, /device:TPU:1, one launch (start us, length us, event | category | flops | bytes accessed | tf_op | source)
XLA Modules:
  0.0 78.0 jit_solution(10289120311361468831)
XLA Ops:
  0.0 0.0 copy-start.3
  0.0 0.0 copy-start
  0.0 0.8 %copy.8.peer = s32[6,4]{1,0:T(8,128)S(1)} copy(s32[6,4]{0,1:T(4,128)} %param.10) | data formatting | bytes 192 | tf_op args[4]
  0.8 0.0 copy-done.3
  0.8 0.1 copy.9.flip
  0.9 0.0 copy-start.2
  0.9 1.0 %copy.7.band_cols = f32[512,25]{1,0:T(8,128)S(1)} copy(f32[512,25]{0,1:T(8,128)} %param.9) | data formatting | bytes 102400 | tf_op args[3]
  1.9 0.0 copy-done
  1.9 0.0 copy-done.2
  1.9 0.0 copy-start.1
  1.9 0.9 %copy-done.1 = f32[6,16,512]{2,1,0:T(8,128)S(1)} copy-done((f32[6,16,512]{2,1,0:T(8,128)S(1)}, f32[6,16,512]{2,1,0:T(8,128)}, u32[]{:S(2)}) %copy-start.1) | copy-done | bytes 196632
  2.9 52.2 %filters.1.part = f32[16,3,8,128]{3,2,1,0:T(8,128)S(1)} custom-call(bf16[2,6,16,512]{3,2,1,0:T(8,128)(2,1)S(1)} %copy-done, f32[6,16,512]{2,1,0:T(8,128)S(1)} %copy-done.1, f32[16,25]{1,0:T(8,128)S(1)} %copy-done.2, f32[512,25]{1,0:T(8,128)S(1)} %copy.7.band_cols, s32[6,4]{1,0:T(8,128)S(1)} %copy.8.peer, s32[6,4]{1,0:T(8,128)S(1)} %copy.9.flip), custom_call_target="tpu_custom_call" | custom-call | tf_op jit(solution)/shard_map/filters/pallas_call | solution.py:520
  55.1 22.2 %member_sum.1 = f32[96,512]{1,0:T(8,128)S(1)} custom-call(f32[16,3,8,128]{3,2,1,0:T(8,128)S(1)} %filters.1.part), custom_call_target="tpu_custom_call" | custom-call | tf_op jit(solution)/shard_map/member_sum/pallas_call | solution.py:557
  77.3 0.7 copy.11
Async XLA Ops:
  0.0 0.8 %copy-start.3 = (s32[6,4]{0,1:T(4,128)S(1)}, s32[6,4]{0,1:T(4,128)}, u32[]{:S(2)}) copy-start(s32[6,4]{0,1:T(4,128)} %param.11) | copy-start | bytes 292
  0.0 1.9 %copy-start = (bf16[2,6,16,512]{3,2,1,0:T(8,128)(2,1)S(1)}, bf16[2,6,16,512]{3,2,1,0:T(8,128)(2,1)}, u32[]{:S(2)}) copy-start(bf16[2,6,16,512]{3,2,1,0:T(8,128)(2,1)} %pert.1) | copy-start | bytes 589828
  0.9 1.0 %copy-start.2 = (f32[16,25]{1,0:T(8,128)S(1)}, f32[16,25]{1,0:T(8,128)}, u32[]{:S(2)}) copy-start(f32[16,25]{1,0:T(8,128)} %band_rows.1) | copy-start | bytes 4804
  1.9 0.9 %copy-start.1 = (f32[6,16,512]{2,1,0:T(8,128)S(1)}, f32[6,16,512]{2,1,0:T(8,128)}, u32[]{:S(2)}) copy-start(f32[6,16,512]{2,1,0:T(8,128)} %control.1) | copy-start | bytes 589828

commit v2 on v1

v2 whole, which is shorter than its diff:
```python
import functools
import math

import jax
import jax.numpy as jnp
import numpy as np
from jax import lax
from jax.experimental import pallas as pl
from jax.experimental.pallas import tpu as pltpu
from jax.sharding import PartitionSpec as P

HALF = 12
ROWS = 16
FACES = 6
LANES = 128
WIDE = 2 * LANES
f32, bf16, i32 = jnp.float32, jnp.bfloat16, jnp.int32


def iota(shape, dim):
    return lax.broadcasted_iota(i32, shape, dim)


def dot(a, b):
    return lax.dot_general(a, b, (((1,), (0,)), ((), ())), preferred_element_type=f32)


def dot_nt(a, b):
    return lax.dot_general(a, b, (((1,), (1,)), ((), ())), preferred_element_type=f32)


def dot_tn(a, b):
    return lax.dot_general(a, b, (((0,), (0,)), ((), ())), preferred_element_type=f32)


def onehot(mask):
    return jnp.where(mask, 1.0, 0.0).astype(bf16)


def taper(band):
    rows, taps = band.shape
    steps = np.arange(2 * HALF + 1, dtype=np.float32) - HALF
    curve = np.exp(-((steps / HALF) ** 2))
    scale = 1.0 / math.sqrt(math.sqrt(float(np.sum(curve * curve))) * float(np.sum(curve)))
    lane = iota((1, taps), 1).astype(f32)
    g = jnp.exp(-(((lane - HALF) / HALF) ** 2)) * scale
    wide = jnp.concatenate([band * g, jnp.zeros((rows, LANES - taps), f32)], axis=1)
    return wide.astype(bf16).astype(f32)


def make_key(member, code, layer, good, other):
    return jnp.where(good, ((member * 24 + code) << 4) + layer, other)


def col_parts(lane):
    face, rest = lane >> 5, lane & 31
    second = rest >= HALF
    layer = jnp.where(second, rest - HALF, rest)
    return face, jnp.where(second, 3, 2), layer, (rest < 2 * HALF) & (face < FACES)


def hub_parts(lane):
    face, layer = (lane & (LANES - 1)) >> 4, lane & 15
    return lane >> 7, face, layer, (face < FACES) & (layer < HALF)


def row_parts(index):
    both = index >> 4
    member = jnp.where(both >= FACES, 1, 0)
    return member, both - FACES * member, index & 15


def halo_parts(index):
    both = (index * 171) >> 11
    member = jnp.where(both >= FACES, 1, 0)
    return member, both - FACES * member, index - both * HALF


def pick_face(face, values):
    out = jnp.zeros(face.shape, i32)
    for f in range(FACES):
        out = jnp.where(face == f, values[f], out)
    return out


def whole_kernel(
    tiles, members, count,
    pert_in, control_in, rows_in, cols_in, peer_in, flip_in, out,
    pert, control, band_rows, band_cols, peer, flip,
    w, wh, halo_s, pa, pall_a, pb, pb_mir, qb, qr_b, pc, pc_mir, pa_c, pall_c, sp, drh, qd, qr_d,
    dmat, xs, zacc, bd, bdh, bdt, bdht, jn, gmat, part, got, mine, done,
    load, ring_s, ring_r, hub_s, hub_r, mir_s, mir_r, sc_s, sc_r, mem_s, mem_r,
):
    T, M = tiles, members
    N = ROWS * T
    NB = N // LANES
    MR, MH = M * FACES * ROWS, M * FACES * HALF
    t, me = lax.axis_index("tile"), lax.axis_index("member")
    prev, nxt, mirror = lax.rem(t + T - 1, T), lax.rem(t + 1, T), T - 1 - t
    hub = jnp.where(t == T - 1, 1, 0)
    is_hub = (t == 0) | (t == T - 1)
    last = hub == 1

    def remote(src, dst, send, recv, where, axis="tile"):
        return pltpu.make_async_remote_copy(
            src_ref=src, dst_ref=dst, send_sem=send, recv_sem=recv,
            device_id={axis: where}, device_id_type=pl.DeviceIdType.MESH,
        )

    def each_tile(act):
        act(lax.rem(t + T // 2, T))

        def body(d, carry):
            act(lax.rem(t + T // 2 + d, T))
            act(lax.rem(t + T // 2 - d, T))
            return carry

        lax.fori_loop(1, T // 2, body, 0)

    barrier = pltpu.get_barrier_semaphore()

    def greet(where, axis="tile"):
        pl.semaphore_signal(
            barrier, inc=1, device_id={axis: where}, device_id_type=pl.DeviceIdType.MESH
        )

    @pl.when(is_hub)
    def _():
        each_tile(greet)

    @pl.when(jnp.logical_not(is_hub))
    def _():
        greet(0)
        greet(T - 1)

    for where in (mirror, prev, nxt):
        greet(where)
    for i in range(1, count):
        greet(lax.rem(me + i, count), "member")

    loads = [
        pltpu.make_async_copy(src, dst, load.at[i])
        for i, (src, dst) in enumerate(
            (
                (pert_in, pert), (control_in, control), (peer_in, peer), (flip_in, flip),
                (rows_in, band_rows), (cols_in, band_cols),
            )
        )
    ]
    for copy in loads:
        copy.start()

    r256, c128 = iota((WIDE, LANES), 0), iota((WIDE, LANES), 1) & 31
    sel = onehot(
        ((r256 < HALF) & (c128 == r256))
        | ((r256 >= WIDE - HALF) & (c128 == HALF + WIDE - 1 - r256))
    )
    group = iota((ROWS, LANES), 1) >> 5
    s0, s1 = iota((MH, MR), 0), iota((MH, MR), 1)
    half_of_row = (s0 * 171) >> 11
    ahead = s1 - (half_of_row << 4) - (s0 - half_of_row * HALF)
    comp = [onehot(ahead == 0), onehot(ahead == ROWS - HALF)]

    def pack(quad):
        packs = []
        for m in range(M):
            blocks = []
            for g in range(2):
                block = jnp.zeros((ROWS, LANES), f32)
                for q in range(4):
                    f = 4 * g + q
                    if f < FACES:
                        at = (m * FACES + f) * ROWS
                        block = jnp.where(group == q, quad[at : at + ROWS], block)
                blocks.append(block)
            packs.append(jnp.concatenate(blocks, axis=1).astype(bf16))
        return packs

    def pack_ends(flat):
        ends = jnp.concatenate([flat[:, :LANES], flat[:, N - LANES :]], axis=1)
        return pack(dot(ends, sel))

    def spread(packs):
        parts = []
        for m in range(M):
            for f in range(FACES):
                g, q = f // 4, f % 4
                block = packs[m][:, g * LANES : (g + 1) * LANES]
                parts.append(jnp.where(group == q, block, 0.0))
        return jnp.concatenate(parts, axis=0).astype(bf16)

    for copy in loads[:4]:
        copy.wait()
    for m in range(M):
        weighted = (pert[m].astype(f32) * control[...]).astype(bf16)
        w[m * FACES * ROWS : (m + 1) * FACES * ROWS, :] = weighted.reshape(FACES * ROWS, N)

    peers = [[peer[e, f] for e in range(4)] for f in range(FACES)]
    flips = [[flip[e, f] for e in range(4)] for f in range(FACES)]
    src_face, src_edge, src_layer, src_good = col_parts(iota((WIDE, WIDE), 0))
    src_cols = make_key(0, 4 * src_face + src_edge, src_layer, src_good, -1)
    lane = iota((WIDE, WIDE), 1)
    _, hub_face, hub_layer, hub_good = hub_parts(lane)
    to_hub = jnp.where(
        lane < LANES,
        pick_face(hub_face, [peers[f][0] for f in range(FACES)]),
        pick_face(hub_face, [peers[f][1] for f in range(FACES)]),
    )
    hub_pick = onehot(src_cols == make_key(0, to_hub, hub_layer, hub_good, -2))

    def hub_messages(packs, dst):
        chosen = [dot(value, hub_pick).astype(bf16) for value in packs]
        for h in range(2):
            for m in range(M):
                dst[h, :, m * LANES : (m + 1) * LANES] = chosen[m][:, h * LANES : (h + 1) * LANES]

    hub_messages(pack_ends(w[...]), pa)
    halo_s[0] = dot(comp[0], w[...]).astype(bf16)
    halo_s[1] = dot(comp[1], w[...]).astype(bf16)

    @pl.when(is_hub)
    def _():
        pl.semaphore_wait(barrier, 3 + T - 1 + count - 1)

    @pl.when(jnp.logical_not(is_hub))
    def _():
        pl.semaphore_wait(barrier, 5 + count - 1)

    def hub_copies(src, dst, base):
        return [
            remote(src.at[h], dst.at[t], hub_s.at[base, h], hub_r.at[base], h * (T - 1))
            for h in range(2)
        ]

    def start_to_hubs(copies):
        for h in range(2):
            @pl.when(t != h * (T - 1))
            def _():
                copies[h].start()

    def finish_to_hubs(copies):
        for h in range(2):
            @pl.when(t != h * (T - 1))
            def _():
                copies[h].wait_send()

    def wait_at_hub(dst, base):
        others = dst.at[pl.ds(0, T - 1)]
        pltpu.make_async_copy(others, others, hub_r.at[base]).wait()

    to_hubs_a = hub_copies(pa, pall_a, 0)
    start_to_hubs(to_hubs_a)
    ring_a = [
        remote(halo_s.at[0], wh.at[1], ring_s.at[0], ring_r.at[0], prev),
        remote(halo_s.at[1], wh.at[0], ring_s.at[1], ring_r.at[1], nxt),
    ]
    for copy in ring_a:
        copy.start()

    for copy in loads[4:]:
        copy.wait()
    lane = iota((LANES, LANES), 1)
    blocks = {}
    for b in range(NB):
        wide = taper(jnp.transpose(band_cols[:, b * LANES : (b + 1) * LANES]))
        wide = jnp.concatenate([wide, jnp.zeros((LANES, LANES), f32)], axis=1)
        wide = pltpu.roll(wide, 0, 1, stride=1, stride_axis=0)
        wide = pltpu.roll(wide, WIDE - HALF, 1)
        over = wide[:, LANES:]
        for c, value in (
            (b, wide[:, :LANES]),
            ((b + 1) % (NB + 1), jnp.where(lane < HALF, over, 0.0)),
            ((b + NB) % (NB + 1), jnp.where(lane >= LANES - HALF, over, 0.0)),
        ):
            blocks[b, c] = blocks[b, c] + value if (b, c) in blocks else value
    from_lane, to_lane = iota((LANES, LANES), 0), iota((LANES, LANES), 1) & 31
    rim_order = onehot(
        ((to_lane < HALF) & (from_lane == LANES - 1 - to_lane))
        | ((to_lane >= HALF) & (to_lane < 2 * HALF) & (from_lane == to_lane - HALF))
    )
    for b in range(NB):
        for c in range(NB + 1):
            value = blocks.get((b, c))
            value = jnp.zeros((LANES, LANES), bf16) if value is None else value.astype(bf16)
            if c == NB:
                value = dot(value, rim_order).astype(bf16)
            dmat[b * LANES : (b + 1) * LANES, c * LANES : (c + 1) * LANES] = value

    base = jnp.concatenate([taper(band_rows[...]), jnp.zeros((ROWS, LANES), f32)], axis=1)
    skew = pltpu.roll(base, ROWS - HALF, 1, stride=1, stride_axis=0)
    skew = skew[:, :LANES].astype(bf16)
    every = jnp.concatenate([skew] * (M * FACES), axis=0)
    tap_at, dst_at = iota((LANES, WIDE), 0), iota((LANES, WIDE), 1)
    row_at, col_at = iota((MR, WIDE), 0) >> 4, iota((MR, WIDE), 1)
    half_at = (dst_at * 171) >> 11
    step_at = dst_at - half_at * HALF

    def banded(expand, same):
        full = jnp.where(same, dot(every, onehot(expand)), 0.0)
        square = jnp.concatenate([full, jnp.zeros((WIDE - MR, WIDE), f32)], axis=0)
        return full, jnp.transpose(square)

    full, turned = banded(tap_at == ROWS + (dst_at & 15), row_at == col_at >> 4)
    bd[...] = full[:, :MR].astype(bf16)
    bdt[...] = turned[:MR, :MR].astype(bf16)
    for side, first in ((0, ROWS - HALF), (1, 2 * ROWS)):
        full, turned = banded(
            (tap_at == first + step_at) & (dst_at < MH), row_at == (col_at * 171) >> 11
        )
        bdh[side] = full[:, :MH].astype(bf16)
        bdht[side] = turned[:MH, :MR].astype(bf16)

    want_face, want_edge, want_layer, want_good = col_parts(iota((WIDE, WIDE), 1))
    want_code = jnp.where(
        want_edge == 2,
        pick_face(want_face, [peers[f][2] for f in range(FACES)]),
        pick_face(want_face, [peers[f][3] for f in range(FACES)]),
    )
    want_turn = jnp.where(
        want_edge == 2,
        pick_face(want_face, [flips[f][2] for f in range(FACES)]),
        pick_face(want_face, [flips[f][3] for f in range(FACES)]),
    )
    want = make_key(0, want_code, want_layer, want_good, -2)
    src_hub, row_face, row_layer, row_good = hub_parts(iota((WIDE, WIDE), 0))
    src_rows = make_key(0, 4 * row_face + src_hub, row_layer, row_good, -1)
    gmat[0] = onehot((src_cols == want) & (want_turn == 0))
    gmat[1] = onehot(src_rows == want)
    gmat[2] = onehot((src_cols == want) & (want_turn == 1))
    back = onehot(iota((ROWS, ROWS), 0) + iota((ROWS, ROWS), 1) == ROWS - 1)

    hub_peers = [jnp.where(last, peers[f][1], peers[f][0]) for f in range(FACES)]
    hub_flips = [jnp.where(last, flips[f][1], flips[f][0]) for f in range(FACES)]

    @pl.when(is_hub)
    def _():
        jn[...] = onehot(iota((N, N), 0) + iota((N, N), 1) == N - 1)

    def flipped(value):
        return dot(value.astype(bf16), jn[...])

    def gather_rows(shape, parts, layer_of, cols, rows):
        def wanted(width):
            index = iota((2 * shape, width), 0)
            turned = index >= shape
            member, face, at = parts(jnp.where(turned, index - shape, index))
            layer = layer_of(at)
            good = (layer < HALF) & ((pick_face(face, hub_flips) == 1) == turned)
            return member, face, layer, good

        total = None
        if cols is not None:
            member, face, layer, good = wanted(WIDE)
            src_m, src_f, src_k, src_ok = hub_parts(iota((2 * shape, WIDE), 1))
            pick = onehot(
                make_key(member, face, layer, good, -2) == make_key(src_m, src_f, src_k, src_ok, -1)
            )
            total = dot_nt(pick, cols[...].reshape(N, WIDE))
        for source, source_parts, source_layer, source_edge in rows:
            member, face, layer, good = wanted(source.shape[0])
            code = pick_face(face, hub_peers)
            src_m, src_f, src_at = source_parts(iota((2 * shape, source.shape[0]), 1))
            src_k = source_layer(src_at)
            pick = onehot(
                make_key(member, code, layer, good, -2)
                == make_key(src_m, 4 * src_f + source_edge, src_k, src_k < HALF, -1)
            )
            value = dot(pick, source)
            total = value if total is None else total + value
        return total[:shape] + flipped(total[shape:])

    def scatter(flat, parts, layer_of, q, qr, base):
        shape = (flat.shape[0], WIDE)
        member, face, at = parts(iota(shape, 0))
        layer = layer_of(at)
        lane = iota(shape, 1)
        here = (layer < HALF) & (lane == member * LANES + (face << 4) + layer)
        turned = pick_face(face, hub_flips) == 1
        value = dot_tn(flat, onehot(here & jnp.logical_not(turned)))
        value = value + dot_tn(flipped(flat).astype(bf16), onehot(here & turned))
        q[...] = value.astype(bf16).reshape(T, ROWS, WIDE)

        def send(there):
            remote(q.at[there], qr.at[hub], sc_s.at[base], sc_r.at[base, hub], there).start()

        each_tile(send)
        qr[hub] = q[t]

    def finish_scatter(q, base):
        others = q.at[pl.ds(0, T - 1)]
        pltpu.make_async_copy(others, others, sc_s.at[base]).wait()

    def wait_scatter(q, qr, base):
        for h in range(2):
            @pl.when(t != h * (T - 1))
            def _():
                remote(
                    q.at[0], qr.at[h], sc_s.at[base], sc_r.at[base, h], h * (T - 1)
                ).wait_recv()

    def arrive_cols(direct, mirrored, qr):
        packs = []
        for m in range(M):
            value = jnp.zeros((ROWS, WIDE), f32)
            if direct is not None:
                value = value + dot(direct[m], gmat[0])
                value = value + dot(back, dot(mirrored[m], gmat[2]).astype(bf16))
            if qr is not None:
                near = [qr[h, :, m * LANES : (m + 1) * LANES] for h in range(2)]
                value = value + dot(jnp.concatenate(near, axis=1), gmat[1])
            packs.append(value)
        return packs

    def forward(at):
        return at

    def by_hub(first, second):
        return lambda at: jnp.where(last, second(at), first(at))

    def back_row(at):
        return ROWS - 1 - at

    def back_halo(at):
        return HALF - 1 - at

    x = dot(bd[...], w[...])
    for copy in ring_a:
        copy.wait_recv()

    @pl.when(is_hub)
    def _():
        pall_a[t] = pa[hub]
        wait_at_hub(pall_a, 0)
        halo = by_hub(back_halo, forward)
        wh[hub] = gather_rows(
            MH, halo_parts, halo, pall_a,
            (
                (w[...], row_parts, by_hub(forward, back_row), hub),
                (wh[hub], halo_parts, halo, 1 - hub),
            ),
        ).astype(bf16)

    x = x + dot(bdh[0], wh[0]) + dot(bdh[1], wh[1])
    xs[:, :N] = x.astype(bf16)

    @pl.when(is_hub)
    def _():
        scatter(xs[:, :N], row_parts, by_hub(forward, back_row), qb, qr_b, 0)

    for m, value in enumerate(pack_ends(xs[:, :N])):
        pb[m] = value
    mirror_b = remote(pb, pb_mir, mir_s.at[0], mir_r.at[0], mirror)
    mirror_b.start()
    mirror_b.wait_recv()
    wait_scatter(qb, qr_b, 0)
    xs[:, N:] = spread(arrive_cols(pb, pb_mir, qr_b))
    y = dot_nt(xs[...], dmat[...]).astype(bf16)

    rims = pack(dot(y, dmat[:, N:]))
    for m, value in enumerate(rims):
        pc[m] = value
    mirror_c = remote(pc, pc_mir, mir_s.at[1], mir_r.at[1], mirror)
    hub_messages(rims, pa_c)
    to_hubs_c = hub_copies(pa_c, pall_c, 1)
    start_to_hubs(to_hubs_c)
    mirror_c.start()
    zacc[...] = dot(y, dmat[:, :N])
    mirror_c.wait_recv()

    @pl.when(is_hub)
    def _():
        pall_c[t] = pa_c[hub]
        wait_at_hub(pall_c, 1)
        zacc[...] += gather_rows(MR, row_parts, by_hub(forward, back_row), pall_c, ())

    ends = dot_nt(spread(arrive_cols(pc, pc_mir, None)), sel)
    zacc[:, :LANES] += ends[:, :LANES]
    zacc[:, N - LANES :] += ends[:, LANES:]

    z = zacc[...].astype(bf16)
    sp[0] = dot(bdht[0], z).astype(bf16)
    sp[1] = dot(bdht[1], z).astype(bf16)
    ring_d = [
        remote(sp.at[0], drh.at[1], ring_s.at[2], ring_r.at[2], prev),
        remote(sp.at[1], drh.at[0], ring_s.at[3], ring_r.at[3], nxt),
    ]

    @pl.when(is_hub)
    def _():
        scatter(sp[hub], halo_parts, by_hub(back_halo, forward), qd, qr_d, 1)

    for copy in ring_d:
        copy.start()
    zacc[...] = dot(bdt[...], z)
    for copy in ring_d:
        copy.wait_recv()

    @pl.when(is_hub)
    def _():
        drh[hub] = gather_rows(
            MH, halo_parts, by_hub(forward, back_halo), None,
            (
                (sp[hub], halo_parts, by_hub(back_halo, forward), hub),
                (drh[hub], halo_parts, by_hub(forward, back_halo), 1 - hub),
            ),
        ).astype(bf16)

    zacc[...] += dot_tn(comp[0], drh[0]) + dot_tn(comp[1], drh[1])
    wait_scatter(qd, qr_d, 1)
    ends = dot_nt(spread(arrive_cols(None, None, qr_d)), sel)
    zacc[:, :LANES] += ends[:, :LANES]
    zacc[:, N - LANES :] += ends[:, LANES:]

    FR = FACES * ROWS
    total = jnp.zeros((FR, N), f32)
    for m in range(M):
        total = total + pert[m].astype(f32).reshape(FR, N) * zacc[m * FR : (m + 1) * FR, :]
    per_chunk = part.shape[1]
    for u in range(count * per_chunk):
        r, c = u // NB, u % NB
        part[u // per_chunk, u % per_chunk] = total[r * 8 : r * 8 + 8, c * LANES : (c + 1) * LANES]

    peers_of_me = [lax.rem(me + i, count) for i in range(1, count)]
    for there in peers_of_me:
        remote(part.at[there], got.at[me], mem_s.at[0], mem_r.at[0], there, "member").start()
    got[me] = part[me]
    others = got.at[pl.ds(0, count - 1)]
    pltpu.make_async_copy(others, others, mem_r.at[0]).wait()
    chunk = got[0]
    for i in range(1, count):
        chunk = chunk + got[i]
    mine[...] = chunk * (1.0 / (M * count - 1.0))
    for there in peers_of_me:
        remote(mine, done.at[me], mem_s.at[1], mem_r.at[1], there, "member").start()
    done[me] = mine[...]
    finished = done.at[pl.ds(0, count - 1)]
    pltpu.make_async_copy(finished, finished, mem_r.at[1]).wait()
    for u in range(count * per_chunk):
        r, c = u // NB, u % NB
        out[r * 8 : r * 8 + 8, c * LANES : (c + 1) * LANES] = done[u // per_chunk, u % per_chunk]

    for copy in ring_a + ring_d + [mirror_b, mirror_c]:
        copy.wait_send()
    finish_to_hubs(to_hubs_a)
    finish_to_hubs(to_hubs_c)

    @pl.when(is_hub)
    def _():
        finish_scatter(qb, 0)
        finish_scatter(qd, 1)

    for i in range(2):
        pltpu.make_async_copy(others, others, mem_s.at[i]).wait()


def per_device(perturbations, control, band_rows, band_cols, edge_peer, edge_flip):
    T, count = lax.axis_size("tile"), lax.axis_size("member")
    M = perturbations.shape[0]
    N = control.shape[-1]
    MR, MH = M * FACES * ROWS, M * FACES * HALF
    per_chunk = FACES * ROWS * N // (8 * LANES) // count
    vmem, hbm = pl.BlockSpec(memory_space=pltpu.VMEM), pl.BlockSpec(memory_space=pltpu.HBM)
    dma = pltpu.SemaphoreType.DMA
    args = (perturbations, control, band_rows, band_cols.T, edge_peer.T, edge_flip.T)
    result = pl.pallas_call(
        functools.partial(whole_kernel, T, M, count),
        out_shape=jax.ShapeDtypeStruct((FACES * ROWS, N), f32),
        in_specs=[hbm] * 6,
        out_specs=vmem,
        scratch_shapes=[
            pltpu.VMEM(args[0].shape, bf16),
            pltpu.VMEM(args[1].shape, f32),
            pltpu.VMEM(args[2].shape, f32),
            pltpu.VMEM(args[3].shape, f32),
            pltpu.SMEM(args[4].shape, i32),
            pltpu.SMEM(args[5].shape, i32),
            pltpu.VMEM((MR, N), bf16),
            pltpu.VMEM((2, MH, N), bf16),
            pltpu.VMEM((2, MH, N), bf16),
            pltpu.VMEM((2, ROWS, WIDE), bf16),
            pltpu.VMEM((T, ROWS, WIDE), bf16),
            pltpu.VMEM((M, ROWS, WIDE), bf16),
            pltpu.VMEM((M, ROWS, WIDE), bf16),
            pltpu.VMEM((T, ROWS, WIDE), bf16),
            pltpu.VMEM((2, ROWS, WIDE), bf16),
            pltpu.VMEM((M, ROWS, WIDE), bf16),
            pltpu.VMEM((M, ROWS, WIDE), bf16),
            pltpu.VMEM((2, ROWS, WIDE), bf16),
            pltpu.VMEM((T, ROWS, WIDE), bf16),
            pltpu.VMEM((2, MH, N), bf16),
            pltpu.VMEM((2, MH, N), bf16),
            pltpu.VMEM((T, ROWS, WIDE), bf16),
            pltpu.VMEM((2, ROWS, WIDE), bf16),
            pltpu.VMEM((N, N + LANES), bf16),
            pltpu.VMEM((MR, N + LANES), bf16),
            pltpu.VMEM((MR, N), f32),
            pltpu.VMEM((MR, MR), bf16),
            pltpu.VMEM((2, MR, MH), bf16),
            pltpu.VMEM((MR, MR), bf16),
            pltpu.VMEM((2, MH, MR), bf16),
            pltpu.VMEM((N, N), bf16),
            pltpu.VMEM((3, WIDE, WIDE), bf16),
            pltpu.VMEM((count, per_chunk, 8, LANES), f32),
            pltpu.VMEM((count, per_chunk, 8, LANES), f32),
            pltpu.VMEM((per_chunk, 8, LANES), f32),
            pltpu.VMEM((count, per_chunk, 8, LANES), f32),
            dma((6,)),
            dma((4,)), dma((4,)),
            dma((2, 2)), dma((2,)),
            dma((2,)), dma((2,)),
            dma((2,)), dma((2, 2)),
            dma((2,)), dma((2,)),
        ],
        compiler_params=pltpu.CompilerParams(
            collective_id=0, has_side_effects=True, vmem_limit_bytes=48 * 1024 * 1024
        ),
        name="covariance",
    )(*args)
    return result.reshape(control.shape)


def solution(mesh):
    return jax.shard_map(
        per_device,
        mesh=mesh,
        in_specs=(
            P("member", None, "tile", None),
            P(None, "tile", None),
            P("tile", None),
            P(),
            P(),
            P(),
        ),
        out_specs=P(None, "tile", None),
        check_vma=False,
    )
```

time: 78.2 us -> 70.1 us (0.90)
  Pallas kernels: 74.4 us -> 65.1 us
  local copies, waits for them, and re-layouts: 3.5 us -> 4.76 us
    pallas_call x2 -> x1, Pallas kernels: 74.4 us -> 65.1 us  [per_device(): pl.pallas_call(functools.partial(whole_kernel, T, M, count), out_shape=ja...]
    unnamed x12 -> x13, local copies, waits for them, and re-layouts: 3.5 us -> 4.76 us
where the time goes in v2:
time: 70.1 us; the launch traced here: 69.9 us
  Pallas kernels  65.1 us (93%)
  local copies, waits for them, and re-layouts  4.76 us (7%)
    pallas_call x1, Pallas kernels, per_device(): pl.pallas_call(functools.partial(whole_kernel, T, M, count), out_shape=ja...  65.1 us
    unnamed x13, local copies, waits for them, and re-layouts  4.76 us

profile of v2, /device:TPU:1, one launch (start us, length us, event | category | flops | bytes accessed | tf_op | source)
XLA Modules:
  0.0 69.9 jit_solution(14337460450940397167)
XLA Ops:
  0.0 0.0 copy-start.5
  0.0 0.0 copy-start.4
  0.0 0.7 copy-done.5
  0.7 0.0 copy-done.4
  0.7 0.0 copy-start
  0.7 0.9 %copy-done = bf16[2,6,16,512]{3,2,1,0:T(8,128)(2,1)S(1)} copy-done((bf16[2,6,16,512]{3,2,1,0:T(8,128)(2,1)S(1)}, bf16[2,6,16,512]{3,2,1,0:T(8,128)(2,1)}, u32[]{:S(2)}) %copy-start) | copy-done | bytes 196632
  1.6 0.0 copy-start.1
  1.6 0.9 %copy-done.1 = f32[6,16,512]{2,1,0:T(8,128)S(1)} copy-done((f32[6,16,512]{2,1,0:T(8,128)S(1)}, f32[6,16,512]{2,1,0:T(8,128)}, u32[]{:S(2)}) %copy-start.1) | copy-done | bytes 196632
  2.6 0.0 copy-start.2
  2.6 0.8 %copy-done.2 = f32[512,25]{0,1:T(8,128)S(1)} copy-done((f32[512,25]{0,1:T(8,128)S(1)}, f32[512,25]{0,1:T(8,128)}, u32[]{:S(2)}) %copy-start.2) | copy-done | bytes 51224
  3.4 0.0 copy-start.3
  3.4 0.7 copy-done.3
  4.1 65.1 %covariance.1 = f32[96,512]{1,0:T(8,128)S(1)} custom-call(bf16[2,6,16,512]{3,2,1,0:T(8,128)(2,1)S(1)} %copy-done, f32[6,16,512]{2,1,0:T(8,128)S(1)} %copy-done.1, f32[16,25]{1,0:T(8,128)S(1)} %copy-done.3, f32[25,512]{1,0:T(8,128)S(1)} %bitcast.5, s32[4,6]{1,0:T(4,128)S(1)} %bitcast.6, s32[4,6]{1,0:T(4,128)S(1)} %bitcast.7), custom_call_target="tpu_custom_call" | custom-call | tf_op jit(solution)/shard_map/covariance/pallas_call | solution.py:565
  69.2 0.7 copy.8
Async XLA Ops:
  0.0 0.7 copy-start.5
  0.0 0.7 copy-start.4
  0.7 0.9 %copy-start = (bf16[2,6,16,512]{3,2,1,0:T(8,128)(2,1)S(1)}, bf16[2,6,16,512]{3,2,1,0:T(8,128)(2,1)}, u32[]{:S(2)}) copy-start(bf16[2,6,16,512]{3,2,1,0:T(8,128)(2,1)} %pert_in.1) | copy-start | bytes 589828
  1.6 0.9 %copy-start.1 = (f32[6,16,512]{2,1,0:T(8,128)S(1)}, f32[6,16,512]{2,1,0:T(8,128)}, u32[]{:S(2)}) copy-start(f32[6,16,512]{2,1,0:T(8,128)} %control_in.1) | copy-start | bytes 589828
  2.6 0.8 %copy-start.2 = (f32[512,25]{0,1:T(8,128)S(1)}, f32[512,25]{0,1:T(8,128)}, u32[]{:S(2)}) copy-start(f32[512,25]{0,1:T(8,128)} %param.9) | copy-start | bytes 153604
  3.4 0.7 copy-start.3

commit v3 on v2

--- a/solution.py
+++ b/solution.py
@@ -87,9 +87,10 @@
     tiles, members, count,
     pert_in, control_in, rows_in, cols_in, peer_in, flip_in, out,
     pert, control, band_rows, band_cols, peer, flip,
-    w, wh, halo_s, pa, pall_a, pb, pb_mir, qb, qr_b, pc, pc_mir, pa_c, pall_c, sp, drh, qd, qr_d,
-    dmat, xs, zacc, bd, bdh, bdt, bdht, jn, gmat, part, got, mine, done,
-    load, ring_s, ring_r, hub_s, hub_r, mir_s, mir_r, sc_s, sc_r, mem_s, mem_r,
+    w, wh, halo_s, pa, pall_a, pw, pw_mir, qw, qr_w, qs, qr_s, pb, pb_mir, qr_b,
+    pc, pc_mir, pa_c, pall_c, qc, qr_c, sp, drh, qd, qr_d,
+    dmat, xs, zacc, bd, bdh, bdt, bdht, jn, gmat, seam, part, got, mine, done,
+    load, ring_s, ring_r, hub_s, hub_r, mir_s, mir_r, strip_s, strip_r, sc_s, sc_r, mem_s, mem_r,
 ):
     T, M = tiles, members
     N = ROWS * T
@@ -97,8 +98,10 @@
     MR, MH = M * FACES * ROWS, M * FACES * HALF
     t, me = lax.axis_index("tile"), lax.axis_index("member")
     prev, nxt, mirror = lax.rem(t + T - 1, T), lax.rem(t + 1, T), T - 1 - t
-    hub = jnp.where(t == T - 1, 1, 0)
+    hub = jnp.where(t >= T // 2, 1, 0)
     is_hub = (t == 0) | (t == T - 1)
+    is_second = (t == 1) | (t == T - 2)
+    inner = jnp.logical_not(is_hub)
     last = hub == 1
 
     def remote(src, dst, send, recv, where, axis="tile"):
@@ -135,6 +138,19 @@
 
     for where in (mirror, prev, nxt):
         greet(where)
+    for second in (1, T - 2):
+        @pl.when(t != second)
+        def _():
+            greet(second)
+
+    beside = []
+    for step in (-1, 1):
+        there = mirror + step
+        beside.append((jnp.clip(there, 0, T - 1), there != t, (there >= 1) & (there <= T - 2)))
+
+        @pl.when(inner & (there != t))
+        def _():
+            greet(there)
     for i in range(1, count):
         greet(lax.rem(me + i, count), "member")
 
@@ -189,7 +205,7 @@
                 parts.append(jnp.where(group == q, block, 0.0))
         return jnp.concatenate(parts, axis=0).astype(bf16)
 
-    for copy in loads[:4]:
+    for copy in loads[:5]:
         copy.wait()
     for m in range(M):
         weighted = (pert[m].astype(f32) * control[...]).astype(bf16)
@@ -214,17 +230,65 @@
             for m in range(M):
                 dst[h, :, m * LANES : (m + 1) * LANES] = chosen[m][:, h * LANES : (h + 1) * LANES]
 
-    hub_messages(pack_ends(w[...]), pa)
+    own_taps = taper(band_rows[...])
+    strips = pack_ends(w[...])
+    hub_messages(strips, pa)
+    for m, value in enumerate(strips):
+        pw[m] = value
+    pw[0, :, LANES:] += pltpu.roll(own_taps, LANES // 2, 1).astype(bf16)
     halo_s[0] = dot(comp[0], w[...]).astype(bf16)
     halo_s[1] = dot(comp[1], w[...]).astype(bf16)
 
-    @pl.when(is_hub)
-    def _():
-        pl.semaphore_wait(barrier, 3 + T - 1 + count - 1)
-
-    @pl.when(jnp.logical_not(is_hub))
-    def _():
-        pl.semaphore_wait(barrier, 5 + count - 1)
+    hub_peers = [jnp.where(last, peers[f][1], peers[f][0]) for f in range(FACES)]
+    hub_flips = [jnp.where(last, flips[f][1], flips[f][0]) for f in range(FACES)]
+
+    def flipped(value):
+        return dot(value.astype(bf16), jn[...])
+
+    def by_hub(first, second):
+        return lambda at: jnp.where(last, second(at), first(at))
+
+    def forward(at):
+        return at
+
+    def back_row(at):
+        return ROWS - 1 - at
+
+    def back_halo(at):
+        return HALF - 1 - at
+
+    def turn_rows(flat, lanes_of):
+        shape = (flat.shape[0], WIDE)
+        member, face, at = row_parts(iota(shape, 0))
+        here = lanes_of(member, face, by_hub(forward, back_row)(at)) == iota(shape, 1)
+        turned = pick_face(face, hub_flips) == 1
+        value = dot_tn(flat, onehot(here & jnp.logical_not(turned)))
+        return value + dot_tn(flipped(flat).astype(bf16), onehot(here & turned))
+
+    @pl.when(is_hub | is_second)
+    def _():
+        jn[...] = onehot(iota((N, N), 0) + iota((N, N), 1) == N - 1)
+
+    @pl.when(is_hub)
+    def _():
+        value = turn_rows(w[...], lambda member, face, at: 96 * member + 16 * face + at)
+        low, high = value[:, :LANES].astype(bf16), value[:, LANES:].astype(bf16)
+        extra = pltpu.roll(own_taps, LANES // 2, 1).astype(bf16)
+        qw[:, :, :LANES] = low.reshape(T, ROWS, LANES)
+        qw[:, :, LANES:] = high.reshape(T, ROWS, LANES) + extra[None]
+
+    @pl.when(is_second)
+    def _():
+        value = turn_rows(
+            w[...],
+            lambda member, face, at: jnp.where(at < 8, 48 * member + 8 * face + at, -1),
+        )
+        qs[...] = value[:, :LANES].astype(bf16).reshape(T, ROWS, LANES)
+
+    greeted = 3 + count - 1 + jnp.where(is_hub, T - 1, 2) + jnp.where(is_second, T - 1, 0)
+    for _, other, inside in beside:
+        greeted = greeted + jnp.where(other & inside, 1, 0)
+    pl.semaphore_wait(barrier, greeted)
 
     def hub_copies(src, dst, base):
         return [
@@ -248,8 +312,39 @@
         others = dst.at[pl.ds(0, T - 1)]
         pltpu.make_async_copy(others, others, hub_r.at[base]).wait()
 
+    def send_all(q, qr, base):
+        def send(there):
+            remote(q.at[there], qr.at[hub], sc_s.at[base], sc_r.at[base, hub], there).start()
+
+        each_tile(send)
+        qr[hub] = q[t]
+
+    def wait_all(q, qr, base, places):
+        for h, place in enumerate(places):
+            @pl.when(t != place)
+            def _():
+                remote(q.at[0], qr.at[h], sc_s.at[base], sc_r.at[base, h], place).wait_recv()
+
     to_hubs_a = hub_copies(pa, pall_a, 0)
     start_to_hubs(to_hubs_a)
+
+    @pl.when(is_hub)
+    def _():
+        send_all(qw, qr_w, 0)
+
+    @pl.when(is_second)
+    def _():
+        send_all(qs, qr_s, 1)
+
+    strip_copies = []
+    middle = (mirror, t >= 0, inner)
+    for i, (there, other, inside) in enumerate((beside[0], middle, beside[1])):
+        strip_copies.append(remote(pw, pw_mir.at[i], strip_s.at[i], strip_r.at[i], there))
+
+        @pl.when(other & inside)
+        def _():
+            strip_copies[i].start()
+
     ring_a = [
         remote(halo_s.at[0], wh.at[1], ring_s.at[0], ring_r.at[0], prev),
         remote(halo_s.at[1], wh.at[0], ring_s.at[1], ring_r.at[1], nxt),
@@ -257,7 +352,7 @@
     for copy in ring_a:
         copy.start()
 
-    for copy in loads[4:]:
+    for copy in loads[5:]:
         copy.wait()
     lane = iota((LANES, LANES), 1)
     blocks = {}
@@ -286,9 +381,12 @@
                 value = dot(value, rim_order).astype(bf16)
             dmat[b * LANES : (b + 1) * LANES, c * LANES : (c + 1) * LANES] = value
 
-    base = jnp.concatenate([taper(band_rows[...]), jnp.zeros((ROWS, LANES), f32)], axis=1)
-    skew = pltpu.roll(base, ROWS - HALF, 1, stride=1, stride_axis=0)
-    skew = skew[:, :LANES].astype(bf16)
+    def skewed(taps, first):
+        wide = jnp.concatenate([taps, jnp.zeros((ROWS, LANES), f32)], axis=1)
+        wide = pltpu.roll(wide, first, 1, stride=1, stride_axis=0)
+        return wide[:, :LANES].astype(bf16)
+
+    skew = skewed(own_taps, ROWS - HALF)
     every = jnp.concatenate([skew] * (M * FACES), axis=0)
     tap_at, dst_at = iota((LANES, WIDE), 0), iota((LANES, WIDE), 1)
     row_at, col_at = iota((MR, WIDE), 0) >> 4, iota((MR, WIDE), 1)
@@ -328,16 +426,6 @@
     gmat[1] = onehot(src_rows == want)
     gmat[2] = onehot((src_cols == want) & (want_turn == 1))
     back = onehot(iota((ROWS, ROWS), 0) + iota((ROWS, ROWS), 1) == ROWS - 1)
-
-    hub_peers = [jnp.where(last, peers[f][1], peers[f][0]) for f in range(FACES)]
-    hub_flips = [jnp.where(last, flips[f][1], flips[f][0]) for f in range(FACES)]
-
-    @pl.when(is_hub)
-    def _():
-        jn[...] = onehot(iota((N, N), 0) + iota((N, N), 1) == N - 1)
-
-    def flipped(value):
-        return dot(value.astype(bf16), jn[...])
 
     def gather_rows(shape, parts, layer_of, cols, rows):
         def wanted(width):
@@ -369,34 +457,9 @@
             total = value if total is None else total + value
         return total[:shape] + flipped(total[shape:])
 
-    def scatter(flat, parts, layer_of, q, qr, base):
-        shape = (flat.shape[0], WIDE)
-        member, face, at = parts(iota(shape, 0))
-        layer = layer_of(at)
-        lane = iota(shape, 1)
-        here = (layer < HALF) & (lane == member * LANES + (face << 4) + layer)
-        turned = pick_face(face, hub_flips) == 1
-        value = dot_tn(flat, onehot(here & jnp.logical_not(turned)))
-        value = value + dot_tn(flipped(flat).astype(bf16), onehot(here & turned))
-        q[...] = value.astype(bf16).reshape(T, ROWS, WIDE)
-
-        def send(there):
-            remote(q.at[there], qr.at[hub], sc_s.at[base], sc_r.at[base, hub], there).start()
-
-        each_tile(send)
-        qr[hub] = q[t]
-
     def finish_scatter(q, base):
         others = q.at[pl.ds(0, T - 1)]
         pltpu.make_async_copy(others, others, sc_s.at[base]).wait()
-
-    def wait_scatter(q, qr, base):
-        for h in range(2):
-            @pl.when(t != h * (T - 1))
-            def _():
-                remote(
-                    q.at[0], qr.at[h], sc_s.at[base], sc_r.at[base, h], h * (T - 1)
-                ).wait_recv()
 
     def arrive_cols(direct, mirrored, qr):
         packs = []
@@ -411,18 +474,6 @@
             packs.append(value)
         return packs
 
-    def forward(at):
-        return at
-
-    def by_hub(first, second):
-        return lambda at: jnp.where(last, second(at), first(at))
-
-    def back_row(at):
-        return ROWS - 1 - at
-
-    def back_halo(at):
-        return HALF - 1 - at
-
     x = dot(bd[...], w[...])
     for copy in ring_a:
         copy.wait_recv()
@@ -443,16 +494,80 @@
     x = x + dot(bdh[0], wh[0]) + dot(bdh[1], wh[1])
     xs[:, :N] = x.astype(bf16)
 
-    @pl.when(is_hub)
-    def _():
-        scatter(xs[:, :N], row_parts, by_hub(forward, back_row), qb, qr_b, 0)
-
     for m, value in enumerate(pack_ends(xs[:, :N])):
         pb[m] = value
     mirror_b = remote(pb, pb_mir, mir_s.at[0], mir_r.at[0], mirror)
-    mirror_b.start()
-    mirror_b.wait_recv()
-    wait_scatter(qb, qr_b, 0)
+
+    @pl.when(is_hub)
+    def _():
+        mirror_b.start()
+
+    wait_all(qw, qr_w, 0, (0, T - 1))
+    wait_all(qs, qr_s, 1, (1, T - 2))
+
+    def sent_taps(block):
+        taps = pltpu.roll(block.astype(f32), LANES // 2, 1)
+        return jnp.where(iota((ROWS, LANES), 1) <= 2 * HALF, taps, 0.0)
+
+    edge_shape = (WIDE + LANES + WIDE, WIDE)
+    index = iota(edge_shape, 0)
+    part_w, part_s = index < WIDE, index < WIDE + LANES
+    low = jnp.where(part_w, index, index - WIDE)
+    arr_m, arr_f, arr_k, arr_ok = hub_parts(index - WIDE - LANES)
+    half_w, half_s = jnp.where(low >= 96, 1, 0), jnp.where(low >= 48, 1, 0)
+    rest_w, rest_s = low - 96 * half_w, low - 48 * half_s
+    src_mf = jnp.where(
+        part_w,
+        jnp.where(low < 192, FACES * half_w + (rest_w >> 4), -1),
+        jnp.where(
+            part_s,
+            jnp.where(low < 96, FACES * half_s + (rest_s >> 3), -1),
+            jnp.where(arr_ok, FACES * arr_m + arr_f, -1),
+        ),
+    )
+    place = jnp.where(
+        part_w,
+        HALF + (rest_w & 15),
+        jnp.where(part_s, HALF + ROWS + (rest_s & 7), HALF - 1 - arr_k),
+    )
+    dst_m, dst_f, dst_k, dst_ok = hub_parts(iota(edge_shape, 1))
+    same = src_mf == jnp.where(dst_ok, FACES * dst_m + dst_f, -2)
+    from_place = onehot(place[:, :LANES] == iota((edge_shape[0], LANES), 1))
+    layer_lane = iota((ROWS, WIDE), 1) & 15
+    to_layer = onehot((iota((ROWS, WIDE), 0) == layer_lane) & (layer_lane < HALF))
+    turn_taps = onehot(
+        (iota((LANES, LANES), 0) + iota((LANES, LANES), 1) == 2 * HALF)
+    )
+    for h in range(2):
+        taps = sent_taps(qr_w[h, :, LANES:])
+        if h == 1:
+            taps = dot(dot(back, taps.astype(bf16)).astype(bf16), turn_taps)
+        by_layer = dot_nt(from_place, skewed(taps, 0)).astype(bf16)
+        seam[h] = jnp.where(same, dot(by_layer, to_layer), 0.0).astype(bf16)
+        line = jnp.concatenate([qr_w[h], qr_s[h], pa[h]], axis=1)
+        qr_b[h] = dot(line, seam[h]).astype(bf16)
+
+    @pl.when(inner)
+    def _():
+        for i, (there, other, inside) in enumerate((beside[0], middle, beside[1])):
+            @pl.when(other)
+            def _():
+                strip_copies[i].wait_recv()
+
+            if i != 1:
+                @pl.when(jnp.logical_not(other))
+                def _():
+                    pw_mir[i] = pw[...]
+
+        mirror_skew = skewed(sent_taps(pw_mir[1, 0, :, LANES:]), ROWS - HALF)
+        for m in range(M):
+            rows = jnp.concatenate([pw_mir[0, m], pw_mir[1, m], pw_mir[2, m]], axis=0)
+            pb_mir[m] = dot(mirror_skew[:, : 3 * ROWS], rows).astype(bf16)
+
+    @pl.when(is_hub)
+    def _():
+        mirror_b.wait_recv()
+
     xs[:, N:] = spread(arrive_cols(pb, pb_mir, qr_b))
     y = dot_nt(xs[...], dmat[...]).astype(bf16)
 
@@ -465,6 +580,18 @@
     start_to_hubs(to_hubs_c)
     mirror_c.start()
     zacc[...] = dot(y, dmat[:, :N])
+
+    @pl.when(is_hub)
+    def _():
+        value = turn_rows(
+            zacc[...].astype(bf16),
+            lambda member, face, at: jnp.where(
+                at < HALF, LANES * member + 16 * face + at, -1
+            ),
+        )
+        qc[...] = value.astype(bf16).reshape(T, ROWS, WIDE)
+        send_all(qc, qr_c, 2)
+
     mirror_c.wait_recv()
 
     @pl.when(is_hub)
@@ -485,12 +612,37 @@
         remote(sp.at[1], drh.at[0], ring_s.at[3], ring_r.at[3], nxt),
     ]
 
-    @pl.when(is_hub)
-    def _():
-        scatter(sp[hub], halo_parts, by_hub(back_halo, forward), qd, qr_d, 1)
-
     for copy in ring_d:
         copy.start()
+
+    wait_all(qc, qr_c, 2, (0, T - 1))
+    hub_d = remote(qd.at[1 - hub], qr_d.at[hub], sc_s.at[3], sc_r.at[3, hub], mirror)
+
+    @pl.when(is_hub)
+    def _():
+        at, end = iota((WIDE, 2 * ROWS), 0), iota((WIDE, 2 * ROWS), 1)
+        ends = onehot(at == jnp.where(end < ROWS, end, end + WIDE - 2 * ROWS))
+        rim = sp[hub]
+        near = dot(jnp.concatenate([rim[:, :LANES], rim[:, N - LANES :]], axis=1), ends)
+        near = near.astype(bf16)
+        mirrored = onehot(iota((2 * ROWS, 2 * ROWS), 0) + iota((2 * ROWS, 2 * ROWS), 1) == 2 * ROWS - 1)
+        shape = (MH, WIDE)
+        member, face, step = halo_parts(iota(shape, 0))
+        layer = by_hub(back_halo, forward)(step)
+        here = iota(shape, 1) == member * LANES + (face << 4) + layer
+        turned = pick_face(face, hub_flips) == 1
+        value = dot_tn(near, onehot(here & jnp.logical_not(turned)))
+        value = value + dot_tn(dot(near, mirrored).astype(bf16), onehot(here & turned))
+        qd[...] = value.astype(bf16).reshape(2, ROWS, WIDE)
+        qr_d[hub] = qd[hub]
+        hub_d.start()
+
+    @pl.when(inner)
+    def _():
+        for h in range(2):
+            strip = (qr_c[h].astype(f32) + pa_c[h].astype(f32)).astype(bf16)
+            qr_d[h] = dot_nt(strip, seam[h, WIDE + LANES :, :]).astype(bf16)
+
     zacc[...] = dot(bdt[...], z)
     for copy in ring_d:
         copy.wait_recv()
@@ -506,7 +658,10 @@
         ).astype(bf16)
 
     zacc[...] += dot_tn(comp[0], drh[0]) + dot_tn(comp[1], drh[1])
-    wait_scatter(qd, qr_d, 1)
+    @pl.when(is_hub)
+    def _():
+        remote(qd.at[0], qr_d.at[1 - hub], sc_s.at[3], sc_r.at[3, 1 - hub], mirror).wait_recv()
+
     ends = dot_nt(spread(arrive_cols(None, None, qr_d)), sel)
     zacc[:, :LANES] += ends[:, :LANES]
     zacc[:, N - LANES :] += ends[:, LANES:]
@@ -539,15 +694,26 @@
         r, c = u // NB, u % NB
         out[r * 8 : r * 8 + 8, c * LANES : (c + 1) * LANES] = done[u // per_chunk, u % per_chunk]
 
-    for copy in ring_a + ring_d + [mirror_b, mirror_c]:
+    for copy in ring_a + ring_d + [mirror_c]:
         copy.wait_send()
+    for i, (there, other, inside) in enumerate((beside[0], middle, beside[1])):
+        @pl.when(other & inside)
+        def _():
+            strip_copies[i].wait_send()
+
     finish_to_hubs(to_hubs_a)
     finish_to_hubs(to_hubs_c)
 
     @pl.when(is_hub)
     def _():
-        finish_scatter(qb, 0)
-        finish_scatter(qd, 1)
+        finish_scatter(qw, 0)
+        finish_scatter(qc, 2)
+        mirror_b.wait_send()
+        hub_d.wait_send()
+
+    @pl.when(is_second)
+    def _():
+        finish_scatter(qs, 1)
 
     for i in range(2):
         pltpu.make_async_copy(others, others, mem_s.at[i]).wait()
@@ -580,16 +746,23 @@
             pltpu.VMEM((2, ROWS, WIDE), bf16),
             pltpu.VMEM((T, ROWS, WIDE), bf16),
             pltpu.VMEM((M, ROWS, WIDE), bf16),
+            pltpu.VMEM((3, M, ROWS, WIDE), bf16),
+            pltpu.VMEM((T, ROWS, WIDE), bf16),
+            pltpu.VMEM((2, ROWS, WIDE), bf16),
+            pltpu.VMEM((T, ROWS, LANES), bf16),
+            pltpu.VMEM((2, ROWS, LANES), bf16),
             pltpu.VMEM((M, ROWS, WIDE), bf16),
-            pltpu.VMEM((T, ROWS, WIDE), bf16),
+            pltpu.VMEM((M, ROWS, WIDE), bf16),
             pltpu.VMEM((2, ROWS, WIDE), bf16),
             pltpu.VMEM((M, ROWS, WIDE), bf16),
             pltpu.VMEM((M, ROWS, WIDE), bf16),
             pltpu.VMEM((2, ROWS, WIDE), bf16),
             pltpu.VMEM((T, ROWS, WIDE), bf16),
+            pltpu.VMEM((T, ROWS, WIDE), bf16),
+            pltpu.VMEM((2, ROWS, WIDE), bf16),
             pltpu.VMEM((2, MH, N), bf16),
             pltpu.VMEM((2, MH, N), bf16),
-            pltpu.VMEM((T, ROWS, WIDE), bf16),
+            pltpu.VMEM((2, ROWS, WIDE), bf16),
             pltpu.VMEM((2, ROWS, WIDE), bf16),
             pltpu.VMEM((N, N + LANES), bf16),
             pltpu.VMEM((MR, N + LANES), bf16),
@@ -600,6 +773,7 @@
             pltpu.VMEM((2, MH, MR), bf16),
             pltpu.VMEM((N, N), bf16),
             pltpu.VMEM((3, WIDE, WIDE), bf16),
+            pltpu.VMEM((2, 2 * WIDE + LANES, WIDE), bf16),
             pltpu.VMEM((count, per_chunk, 8, LANES), f32),
             pltpu.VMEM((count, per_chunk, 8, LANES), f32),
             pltpu.VMEM((per_chunk, 8, LANES), f32),
@@ -608,11 +782,12 @@
             dma((4,)), dma((4,)),
             dma((2, 2)), dma((2,)),
             dma((2,)), dma((2,)),
-            dma((2,)), dma((2, 2)),
+            dma((3,)), dma((3,)),
+            dma((4,)), dma((4, 2)),
             dma((2,)), dma((2,)),
         ],
         compiler_params=pltpu.CompilerParams(
-            collective_id=0, has_side_effects=True, vmem_limit_bytes=48 * 1024 * 1024
+            collective_id=0, has_side_effects=True, vmem_limit_bytes=60 * 1024 * 1024
         ),
         name="covariance",
     )(*args)

time: 70.1 us -> 60.6 us (0.86)
  Pallas kernels: 65.1 us -> 58.8 us
  local copies, waits for them, and re-layouts: 4.76 us -> 1.62 us
    pallas_call x1, Pallas kernels: 65.1 us -> 58.8 us  [per_device(): pl.pallas_call(functools.partial(whole_kernel, T, M, count), out_shape=ja...]
    unnamed x13 -> x1, local copies, waits for them, and re-layouts: 4.76 us -> 1.62 us
where the time goes in v3:
time: 60.6 us; the launch traced here: 60.4 us
  Pallas kernels  58.8 us (97%)
  local copies, waits for them, and re-layouts  1.62 us (3%)
    pallas_call x1, Pallas kernels, per_device(): pl.pallas_call(functools.partial(whole_kernel, T, M, count), out_shape=ja...  58.8 us
    unnamed x1, local copies, waits for them, and re-layouts  1.62 us

profile of v3, /device:TPU:1, one launch (start us, length us, event | category | flops | bytes accessed | tf_op | source)
XLA Modules:
  0.0 60.4 jit_solution(8908733105466100703)
XLA Ops:
  0.0 58.8 %covariance.1 = f32[96,512]{1,0:T(8,128)} custom-call(bf16[2,6,16,512]{3,2,1,0:T(8,128)(2,1)} %pert_in.1, f32[6,16,512]{2,1,0:T(8,128)} %control_in.1, f32[16,25]{1,0:T(8,128)} %rows_in.1, f32[25,512]{1,0:T(8,128)} %bitcast.5, s32[4,6]{1,0:T(4,128)} %bitcast.6, s32[4,6]{1,0:T(4,128)} %bitcast.7), custom_call_target="tpu_custom_call" | custom-call | tf_op jit(solution)/shard_map/covariance/pallas_call | solution.py:731
  58.8 1.6 %copy.8 = f32[6,16,512]{2,1,0:T(8,128)} copy(f32[6,16,512]{2,1,0:T(8,128)} %bitcast.4) | data formatting | bytes 393216

commit v4 on v3

--- a/solution.py
+++ b/solution.py
@@ -88,7 +88,7 @@
     pert_in, control_in, rows_in, cols_in, peer_in, flip_in, out,
     pert, control, band_rows, band_cols, peer, flip,
     w, wh, halo_s, pa, pall_a, pw, pw_mir, qw, qr_w, qs, qr_s, pb, pb_mir, qr_b,
-    pc, pc_mir, pa_c, pall_c, qc, qr_c, sp, drh, qd, qr_d,
+    pc, pc_mir, pa_c, pall_c, qc, qc_near, qr_c, sp, drh, late, late_r, qd, qr_d,
     dmat, xs, zacc, bd, bdh, bdt, bdht, jn, gmat, seam, part, got, mine, done,
     load, ring_s, ring_r, hub_s, hub_r, mir_s, mir_r, strip_s, strip_r, sc_s, sc_r, mem_s, mem_r,
 ):
@@ -498,9 +498,22 @@
         pb[m] = value
     mirror_b = remote(pb, pb_mir, mir_s.at[0], mir_r.at[0], mirror)
 
+    def to_strips(member, face, at):
+        return jnp.where(at < HALF, LANES * member + 16 * face + at, -1)
+
     @pl.when(is_hub)
     def _():
         mirror_b.start()
+        rough = dot_nt(xs[:, :N], dmat[:, :N]).astype(bf16)
+        value = turn_rows(dot(rough, dmat[:, :N]).astype(bf16), to_strips)
+        qc[...] = value.astype(bf16).reshape(T, ROWS, WIDE)
+
+        def send(there):
+            @pl.when((there > 1) & (there < T - 2))
+            def _():
+                remote(qc.at[there], qr_c.at[hub], sc_s.at[2], sc_r.at[2, hub], there).start()
+
+        each_tile(send)
 
     wait_all(qw, qr_w, 0, (0, T - 1))
     wait_all(qs, qr_s, 1, (1, T - 2))
@@ -581,83 +594,122 @@
     mirror_c.start()
     zacc[...] = dot(y, dmat[:, :N])
 
-    @pl.when(is_hub)
-    def _():
-        value = turn_rows(
-            zacc[...].astype(bf16),
-            lambda member, face, at: jnp.where(
-                at < HALF, LANES * member + 16 * face + at, -1
-            ),
+    def end_columns(flat, width):
+        at, end = iota((WIDE, 2 * width), 0), iota((WIDE, 2 * width), 1)
+        pick = onehot(at == jnp.where(end < width, end, end + WIDE - 2 * width))
+        both = iota((2 * width, 2 * width), 0) + iota((2 * width, 2 * width), 1)
+        near = jnp.concatenate([flat[:, :LANES], flat[:, N - LANES :]], axis=1)
+        near = dot(near, pick).astype(bf16)
+        return near, dot(near, onehot(both == 2 * width - 1)).astype(bf16)
+
+    def near_strips(flat, width, parts, layer_of, lanes_of):
+        near, far = end_columns(flat, width)
+        shape = (flat.shape[0], WIDE)
+        member, face, at = parts(iota(shape, 0))
+        here = lanes_of(member, face, layer_of(at)) == iota(shape, 1)
+        turned = pick_face(face, hub_flips) == 1
+        value = dot_tn(near, onehot(here & jnp.logical_not(turned)))
+        value = value + dot_tn(far, onehot(here & turned))
+        return value.astype(bf16).reshape(2 * width // ROWS, ROWS, WIDE)
+
+    @pl.when(is_hub)
+    def _():
+        qc_near[...] = near_strips(
+            zacc[...].astype(bf16), 2 * ROWS, row_parts, by_hub(forward, back_row), to_strips
         )
-        qc[...] = value.astype(bf16).reshape(T, ROWS, WIDE)
-        send_all(qc, qr_c, 2)
-
-    mirror_c.wait_recv()
-
-    @pl.when(is_hub)
-    def _():
-        pall_c[t] = pa_c[hub]
-        wait_at_hub(pall_c, 1)
-        zacc[...] += gather_rows(MR, row_parts, by_hub(forward, back_row), pall_c, ())
-
-    ends = dot_nt(spread(arrive_cols(pc, pc_mir, None)), sel)
-    zacc[:, :LANES] += ends[:, :LANES]
-    zacc[:, N - LANES :] += ends[:, LANES:]
-
-    z = zacc[...].astype(bf16)
-    sp[0] = dot(bdht[0], z).astype(bf16)
-    sp[1] = dot(bdht[1], z).astype(bf16)
+        for i, there in ((1, 1), (2, T - 2)):
+            remote(
+                qc_near.at[i], qr_c.at[hub], sc_s.at[3 + i], sc_r.at[2, hub], there
+            ).start()
+
     ring_d = [
         remote(sp.at[0], drh.at[1], ring_s.at[2], ring_r.at[2], prev),
         remote(sp.at[1], drh.at[0], ring_s.at[3], ring_r.at[3], nxt),
     ]
-
-    for copy in ring_d:
-        copy.start()
-
-    wait_all(qc, qr_c, 2, (0, T - 1))
+    ring_late = [
+        remote(late.at[0], late_r.at[1], ring_s.at[4], ring_r.at[4], prev),
+        remote(late.at[1], late_r.at[0], ring_s.at[5], ring_r.at[5], nxt),
+    ]
+
+    def start_spills(value):
+        for side in range(2):
+            sp[side] = dot(bdht[side], value).astype(bf16)
+            ring_d[side].start()
+
+    @pl.when(inner)
+    def _():
+        start_spills(zacc[...].astype(bf16))
+
+    mirror_c.wait_recv()
+
+    @pl.when(is_hub)
+    def _():
+        pall_c[t] = pa_c[hub]
+        wait_at_hub(pall_c, 1)
+        zacc[...] += gather_rows(MR, row_parts, by_hub(forward, back_row), pall_c, ())
+
+    ends = dot_nt(spread(arrive_cols(pc, pc_mir, None)), sel)
+    zacc[:, :LANES] += ends[:, :LANES]
+    zacc[:, N - LANES :] += ends[:, LANES:]
+
+    z = zacc[...].astype(bf16)
+    quarter = iota((MH, LANES), 1) >> 5
+
+    def both_ends(value):
+        return dot(jnp.concatenate([value[:, :LANES], value[:, N - LANES :]], axis=1), sel)
+
+    z_ends = both_ends(z).astype(bf16)
+    for side in range(2):
+        value = dot(bdht[side], z_ends)
+        late[side] = jnp.where(quarter == 1 - side, value, 0.0).astype(bf16)
+        ring_late[side].start()
+
+    @pl.when(is_hub)
+    def _():
+        start_spills(z)
+
     hub_d = remote(qd.at[1 - hub], qr_d.at[hub], sc_s.at[3], sc_r.at[3, hub], mirror)
 
     @pl.when(is_hub)
     def _():
-        at, end = iota((WIDE, 2 * ROWS), 0), iota((WIDE, 2 * ROWS), 1)
-        ends = onehot(at == jnp.where(end < ROWS, end, end + WIDE - 2 * ROWS))
-        rim = sp[hub]
-        near = dot(jnp.concatenate([rim[:, :LANES], rim[:, N - LANES :]], axis=1), ends)
-        near = near.astype(bf16)
-        mirrored = onehot(iota((2 * ROWS, 2 * ROWS), 0) + iota((2 * ROWS, 2 * ROWS), 1) == 2 * ROWS - 1)
-        shape = (MH, WIDE)
-        member, face, step = halo_parts(iota(shape, 0))
-        layer = by_hub(back_halo, forward)(step)
-        here = iota(shape, 1) == member * LANES + (face << 4) + layer
-        turned = pick_face(face, hub_flips) == 1
-        value = dot_tn(near, onehot(here & jnp.logical_not(turned)))
-        value = value + dot_tn(dot(near, mirrored).astype(bf16), onehot(here & turned))
-        qd[...] = value.astype(bf16).reshape(2, ROWS, WIDE)
+        qd[...] = near_strips(
+            sp[hub], ROWS, halo_parts, by_hub(back_halo, forward),
+            lambda member, face, at: LANES * member + 16 * face + at,
+        )
         qr_d[hub] = qd[hub]
         hub_d.start()
 
+    zacc[...] = dot(bdt[...], z)
+
     @pl.when(inner)
     def _():
+        wait_all(qc, qr_c, 2, (0, T - 1))
         for h in range(2):
             strip = (qr_c[h].astype(f32) + pa_c[h].astype(f32)).astype(bf16)
             qr_d[h] = dot_nt(strip, seam[h, WIDE + LANES :, :]).astype(bf16)
 
-    zacc[...] = dot(bdt[...], z)
-    for copy in ring_d:
+    for copy in ring_d + ring_late:
         copy.wait_recv()
 
     @pl.when(is_hub)
     def _():
-        drh[hub] = gather_rows(
+        arrived = gather_rows(
             MH, halo_parts, by_hub(forward, back_halo), None,
             (
                 (sp[hub], halo_parts, by_hub(back_halo, forward), hub),
                 (drh[hub], halo_parts, by_hub(forward, back_halo), 1 - hub),
             ),
         ).astype(bf16)
-
-    zacc[...] += dot_tn(comp[0], drh[0]) + dot_tn(comp[1], drh[1])
+        drh[hub] = arrived
+        late_r[hub] = jnp.where(quarter == hub, both_ends(arrived), 0.0).astype(bf16)
+
+    spill = dot_tn(comp[0], drh[0]) + dot_tn(comp[1], drh[1])
+    column = iota((MR, N), 1)
+    zacc[...] += jnp.where((column >= HALF) & (column < N - HALF), spill, 0.0)
+    spill_ends = dot_tn(comp[0], late_r[0]) + dot_tn(comp[1], late_r[1])
+    ends = dot_nt(spill_ends.astype(bf16), sel)
+    zacc[:, :LANES] += ends[:, :LANES]
+    zacc[:, N - LANES :] += ends[:, LANES:]
     @pl.when(is_hub)
     def _():
         remote(qd.at[0], qr_d.at[1 - hub], sc_s.at[3], sc_r.at[3, 1 - hub], mirror).wait_recv()
@@ -694,7 +746,7 @@
         r, c = u // NB, u % NB
         out[r * 8 : r * 8 + 8, c * LANES : (c + 1) * LANES] = done[u // per_chunk, u % per_chunk]
 
-    for copy in ring_a + ring_d + [mirror_c]:
+    for copy in ring_a + ring_d + ring_late + [mirror_c]:
         copy.wait_send()
     for i, (there, other, inside) in enumerate((beside[0], middle, beside[1])):
         @pl.when(other & inside)
@@ -707,7 +759,10 @@
     @pl.when(is_hub)
     def _():
         finish_scatter(qw, 0)
-        finish_scatter(qc, 2)
+        far = qc.at[pl.ds(0, T - 4)]
+        pltpu.make_async_copy(far, far, sc_s.at[2]).wait()
+        for i in (1, 2):
+            remote(qc_near.at[i], qr_c.at[hub], sc_s.at[3 + i], sc_r.at[2, hub], 1).wait_send()
         mirror_b.wait_send()
         hub_d.wait_send()
 
@@ -759,9 +814,12 @@
             pltpu.VMEM((2, ROWS, WIDE), bf16),
             pltpu.VMEM((T, ROWS, WIDE), bf16),
             pltpu.VMEM((T, ROWS, WIDE), bf16),
+            pltpu.VMEM((4, ROWS, WIDE), bf16),
             pltpu.VMEM((2, ROWS, WIDE), bf16),
             pltpu.VMEM((2, MH, N), bf16),
             pltpu.VMEM((2, MH, N), bf16),
+            pltpu.VMEM((2, MH, LANES), bf16),
+            pltpu.VMEM((2, MH, LANES), bf16),
             pltpu.VMEM((2, ROWS, WIDE), bf16),
             pltpu.VMEM((2, ROWS, WIDE), bf16),
             pltpu.VMEM((N, N + LANES), bf16),
@@ -779,11 +837,11 @@
             pltpu.VMEM((per_chunk, 8, LANES), f32),
             pltpu.VMEM((count, per_chunk, 8, LANES), f32),
             dma((6,)),
-            dma((4,)), dma((4,)),
+            dma((6,)), dma((6,)),
             dma((2, 2)), dma((2,)),
             dma((2,)), dma((2,)),
             dma((3,)), dma((3,)),
-            dma((4,)), dma((4, 2)),
+            dma((6,)), dma((4, 2)),
             dma((2,)), dma((2,)),
         ],
         compiler_params=pltpu.CompilerParams(

time: 60.6 us -> 61.5 us (1.015)
  Pallas kernels: 58.8 us -> 59.7 us
    pallas_call x1, Pallas kernels: 58.8 us -> 59.7 us  [per_device(): pl.pallas_call(functools.partial(whole_kernel, T, M, count), out_shape=ja...]
where the time goes in v4:
time: 61.5 us; the launch traced here: 61.3 us
  Pallas kernels  59.7 us (97%)
  local copies, waits for them, and re-layouts  1.62 us (3%)
    pallas_call x1, Pallas kernels, per_device(): pl.pallas_call(functools.partial(whole_kernel, T, M, count), out_shape=ja...  59.7 us
    unnamed x1, local copies, waits for them, and re-layouts  1.62 us

profile of v4, /device:TPU:1, one launch (start us, length us, event | category | flops | bytes accessed | tf_op | source)
XLA Modules:
  0.0 61.3 jit_solution(14657140439984709701)
XLA Ops:
  0.0 59.7 %covariance.1 = f32[96,512]{1,0:T(8,128)} custom-call(bf16[2,6,16,512]{3,2,1,0:T(8,128)(2,1)} %pert_in.1, f32[6,16,512]{2,1,0:T(8,128)} %control_in.1, f32[16,25]{1,0:T(8,128)} %rows_in.1, f32[25,512]{1,0:T(8,128)} %bitcast.5, s32[4,6]{1,0:T(4,128)} %bitcast.6, s32[4,6]{1,0:T(4,128)} %bitcast.7), custom_call_target="tpu_custom_call" | custom-call | tf_op jit(solution)/shard_map/covariance/pallas_call | solution.py:786
  59.7 1.6 %copy.8 = f32[6,16,512]{2,1,0:T(8,128)} copy(f32[6,16,512]{2,1,0:T(8,128)} %bitcast.4) | data formatting | bytes 393216

commit v5 on v4

--- a/solution.py
+++ b/solution.py
@@ -88,8 +88,8 @@
     pert_in, control_in, rows_in, cols_in, peer_in, flip_in, out,
     pert, control, band_rows, band_cols, peer, flip,
     w, wh, halo_s, pa, pall_a, pw, pw_mir, qw, qr_w, qs, qr_s, pb, pb_mir, qr_b,
-    pc, pc_mir, pa_c, pall_c, qc, qc_near, qr_c, sp, drh, late, late_r, qd, qr_d,
-    dmat, xs, zacc, bd, bdh, bdt, bdht, jn, gmat, seam, part, got, mine, done,
+    pc, pc_mir, pa_c, pall_c, qc, qr_c, sp, drh, late, late_r, qd, qr_d,
+    dmat, xs, zacc, bd, bdh, bdt, bdht, jn, gmat, seam, seam_mask, from_place, picks, part, got, mine, done,
     load, ring_s, ring_r, hub_s, hub_r, mir_s, mir_r, strip_s, strip_r, sc_s, sc_r, mem_s, mem_r,
 ):
     T, M = tiles, members
@@ -236,14 +236,21 @@
     for m, value in enumerate(strips):
         pw[m] = value
     pw[0, :, LANES:] += pltpu.roll(own_taps, LANES // 2, 1).astype(bf16)
-    halo_s[0] = dot(comp[0], w[...]).astype(bf16)
-    halo_s[1] = dot(comp[1], w[...]).astype(bf16)
+
+    def end_blocks(flat):
+        return jnp.concatenate([flat[:, :LANES], flat[:, N - LANES :]], axis=1)
+
+    for side in range(2):
+        rows = dot(comp[side], w[...]).astype(bf16)
+        halo_s[side, 0] = end_blocks(rows)
+        halo_s[side, 1] = rows[:, LANES : N - LANES]
 
     hub_peers = [jnp.where(last, peers[f][1], peers[f][0]) for f in range(FACES)]
     hub_flips = [jnp.where(last, flips[f][1], flips[f][0]) for f in range(FACES)]
 
     def flipped(value):
-        return dot(value.astype(bf16), jn[...])
+        width = value.shape[1]
+        return dot(value.astype(bf16), jn[:width, N - width :])
 
     def by_hub(first, second):
         return lambda at: jnp.where(last, second(at), first(at))
@@ -345,9 +352,15 @@
         def _():
             strip_copies[i].start()
 
-    ring_a = [
-        remote(halo_s.at[0], wh.at[1], ring_s.at[0], ring_r.at[0], prev),
-        remote(halo_s.at[1], wh.at[0], ring_s.at[1], ring_r.at[1], nxt),
+    ring_a, ring_mid = [
+        [
+            remote(
+                halo_s.at[side, part], wh.at[1 - side, part],
+                ring_s.at[2 * part + side], ring_r.at[2 * part + side], (prev, nxt)[side],
+            )
+            for side in range(2)
+        ]
+        for part in range(2)
     ]
     for copy in ring_a:
         copy.start()
@@ -427,7 +440,7 @@
     gmat[2] = onehot((src_cols == want) & (want_turn == 1))
     back = onehot(iota((ROWS, ROWS), 0) + iota((ROWS, ROWS), 1) == ROWS - 1)
 
-    def gather_rows(shape, parts, layer_of, cols, rows):
+    def hub_picks(slot, shape, parts, layer_of, cols, rows):
         def wanted(width):
             index = iota((2 * shape, width), 0)
             turned = index >= shape
@@ -436,25 +449,33 @@
             good = (layer < HALF) & ((pick_face(face, hub_flips) == 1) == turned)
             return member, face, layer, good
 
-        total = None
-        if cols is not None:
+        if cols:
             member, face, layer, good = wanted(WIDE)
             src_m, src_f, src_k, src_ok = hub_parts(iota((2 * shape, WIDE), 1))
-            pick = onehot(
+            picks[slot, : 2 * shape] = onehot(
                 make_key(member, face, layer, good, -2) == make_key(src_m, src_f, src_k, src_ok, -1)
             )
-            total = dot_nt(pick, cols[...].reshape(N, WIDE))
-        for source, source_parts, source_layer, source_edge in rows:
-            member, face, layer, good = wanted(source.shape[0])
+            slot += 1
+        for width, source_parts, source_layer, source_edge in rows:
+            member, face, layer, good = wanted(width)
             code = pick_face(face, hub_peers)
-            src_m, src_f, src_at = source_parts(iota((2 * shape, source.shape[0]), 1))
+            src_m, src_f, src_at = source_parts(iota((2 * shape, width), 1))
             src_k = source_layer(src_at)
-            pick = onehot(
+            picks[slot, : 2 * shape, :width] = onehot(
                 make_key(member, code, layer, good, -2)
                 == make_key(src_m, 4 * src_f + source_edge, src_k, src_k < HALF, -1)
             )
-            value = dot(pick, source)
+            slot += 1
+
+    def gather_rows(slot, shape, cols, rows):
+        total = None
+        if cols is not None:
+            total = dot_nt(picks[slot, : 2 * shape], cols)
+            slot += 1
+        for source in rows:
+            value = dot(picks[slot, : 2 * shape, : source.shape[0]], source)
             total = value if total is None else total + value
+            slot += 1
         return total[:shape] + flipped(total[shape:])
 
     def finish_scatter(q, base):
@@ -474,53 +495,16 @@
             packs.append(value)
         return packs
 
-    x = dot(bd[...], w[...])
-    for copy in ring_a:
-        copy.wait_recv()
-
-    @pl.when(is_hub)
-    def _():
-        pall_a[t] = pa[hub]
-        wait_at_hub(pall_a, 0)
-        halo = by_hub(back_halo, forward)
-        wh[hub] = gather_rows(
-            MH, halo_parts, halo, pall_a,
-            (
-                (w[...], row_parts, by_hub(forward, back_row), hub),
-                (wh[hub], halo_parts, halo, 1 - hub),
-            ),
-        ).astype(bf16)
-
-    x = x + dot(bdh[0], wh[0]) + dot(bdh[1], wh[1])
-    xs[:, :N] = x.astype(bf16)
-
-    for m, value in enumerate(pack_ends(xs[:, :N])):
-        pb[m] = value
-    mirror_b = remote(pb, pb_mir, mir_s.at[0], mir_r.at[0], mirror)
-
-    def to_strips(member, face, at):
-        return jnp.where(at < HALF, LANES * member + 16 * face + at, -1)
-
-    @pl.when(is_hub)
-    def _():
-        mirror_b.start()
-        rough = dot_nt(xs[:, :N], dmat[:, :N]).astype(bf16)
-        value = turn_rows(dot(rough, dmat[:, :N]).astype(bf16), to_strips)
-        qc[...] = value.astype(bf16).reshape(T, ROWS, WIDE)
-
-        def send(there):
-            @pl.when((there > 1) & (there < T - 2))
-            def _():
-                remote(qc.at[there], qr_c.at[hub], sc_s.at[2], sc_r.at[2, hub], there).start()
-
-        each_tile(send)
-
-    wait_all(qw, qr_w, 0, (0, T - 1))
-    wait_all(qs, qr_s, 1, (1, T - 2))
-
-    def sent_taps(block):
-        taps = pltpu.roll(block.astype(f32), LANES // 2, 1)
-        return jnp.where(iota((ROWS, LANES), 1) <= 2 * HALF, taps, 0.0)
+    halo_near, halo_far = by_hub(forward, back_halo), by_hub(back_halo, forward)
+    edge_rows = by_hub(forward, back_row)
+
+    @pl.when(is_hub)
+    def _():
+        rows = ((MR, row_parts, edge_rows, hub), (MH, halo_parts, halo_far, 1 - hub))
+        hub_picks(0, MH, halo_parts, halo_far, True, rows)
+        hub_picks(3, MR, row_parts, edge_rows, True, ())
+        rows = ((MH, halo_parts, halo_far, hub), (MH, halo_parts, halo_near, 1 - hub))
+        hub_picks(4, MH, halo_parts, halo_near, False, rows)
 
     edge_shape = (WIDE + LANES + WIDE, WIDE)
     index = iota(edge_shape, 0)
@@ -545,18 +529,27 @@
     )
     dst_m, dst_f, dst_k, dst_ok = hub_parts(iota(edge_shape, 1))
     same = src_mf == jnp.where(dst_ok, FACES * dst_m + dst_f, -2)
-    from_place = onehot(place[:, :LANES] == iota((edge_shape[0], LANES), 1))
+    seam_mask[...] = jnp.where(same, 1.0, 0.0)
+    from_place[...] = onehot(place[:, :LANES] == iota((edge_shape[0], LANES), 1))
     layer_lane = iota((ROWS, WIDE), 1) & 15
     to_layer = onehot((iota((ROWS, WIDE), 0) == layer_lane) & (layer_lane < HALF))
     turn_taps = onehot(
         (iota((LANES, LANES), 0) + iota((LANES, LANES), 1) == 2 * HALF)
     )
+
+    wait_all(qw, qr_w, 0, (0, T - 1))
+    wait_all(qs, qr_s, 1, (1, T - 2))
+
+    def sent_taps(block):
+        taps = pltpu.roll(block.astype(f32), LANES // 2, 1)
+        return jnp.where(iota((ROWS, LANES), 1) <= 2 * HALF, taps, 0.0)
+
     for h in range(2):
         taps = sent_taps(qr_w[h, :, LANES:])
         if h == 1:
             taps = dot(dot(back, taps.astype(bf16)).astype(bf16), turn_taps)
-        by_layer = dot_nt(from_place, skewed(taps, 0)).astype(bf16)
-        seam[h] = jnp.where(same, dot(by_layer, to_layer), 0.0).astype(bf16)
+        by_layer = dot_nt(from_place[...], skewed(taps, 0)).astype(bf16)
+        seam[h] = (dot(by_layer, to_layer) * seam_mask[...]).astype(bf16)
         line = jnp.concatenate([qr_w[h], qr_s[h], pa[h]], axis=1)
         qr_b[h] = dot(line, seam[h]).astype(bf16)
 
@@ -577,14 +570,47 @@
             rows = jnp.concatenate([pw_mir[0, m], pw_mir[1, m], pw_mir[2, m]], axis=0)
             pb_mir[m] = dot(mirror_skew[:, : 3 * ROWS], rows).astype(bf16)
 
-    @pl.when(is_hub)
-    def _():
+    x = dot(bd[...], w[...])
+    for copy in ring_a:
+        copy.wait_recv()
+    for copy in ring_mid:
+        copy.start()
+    side_tiles = LANES // ROWS
+
+    @pl.when(is_hub)
+    def _():
+        pall_a[t] = pa[hub]
+        wait_at_hub(pall_a, 0)
+        near = jnp.concatenate([pall_a[:side_tiles], pall_a[T - side_tiles :]], axis=0)
+        wh[hub, 0] = gather_rows(
+            0, MH, near.reshape(WIDE, WIDE), (end_blocks(w[...]), wh[hub, 0])
+        ).astype(bf16)
+
+    x_ends = (end_blocks(x) + dot(bdh[0], wh[0, 0]) + dot(bdh[1], wh[1, 0])).astype(bf16)
+    xs[:, :LANES] = x_ends[:, :LANES]
+    xs[:, N - LANES : N] = x_ends[:, LANES:]
+
+    for m, value in enumerate(pack_ends(xs[:, :N])):
+        pb[m] = value
+    mirror_b = remote(pb, pb_mir, mir_s.at[0], mir_r.at[0], mirror)
+
+    def to_strips(member, face, at):
+        return jnp.where(at < HALF, LANES * member + 16 * face + at, -1)
+
+    @pl.when(is_hub)
+    def _():
+        mirror_b.start()
         mirror_b.wait_recv()
 
     xs[:, N:] = spread(arrive_cols(pb, pb_mir, qr_b))
-    y = dot_nt(xs[...], dmat[...]).astype(bf16)
-
-    rims = pack(dot(y, dmat[:, N:]))
+
+    zrim = jnp.zeros((MR, LANES), f32)
+    for at in (0, N - LANES):
+        here = slice(at, at + LANES)
+        value = jnp.concatenate([xs[:, here], xs[:, N:]], axis=1)
+        weights = jnp.concatenate([dmat[here, here], dmat[here, N:]], axis=1)
+        zrim = zrim + dot(dot_nt(value, weights).astype(bf16), dmat[here, N:])
+    rims = pack(zrim)
     for m, value in enumerate(rims):
         pc[m] = value
     mirror_c = remote(pc, pc_mir, mir_s.at[1], mir_r.at[1], mirror)
@@ -592,6 +618,20 @@
     to_hubs_c = hub_copies(pa_c, pall_c, 1)
     start_to_hubs(to_hubs_c)
     mirror_c.start()
+
+    for copy in ring_mid:
+        copy.wait_recv()
+
+    @pl.when(is_hub)
+    def _():
+        middle_cols = pall_a[side_tiles : T - side_tiles].reshape(N - WIDE, WIDE)
+        wh[hub, 1] = gather_rows(
+            0, MH, middle_cols, (w[:, LANES : N - LANES], wh[hub, 1])
+        ).astype(bf16)
+
+    x_mid = x[:, LANES : N - LANES] + dot(bdh[0], wh[0, 1]) + dot(bdh[1], wh[1, 1])
+    xs[:, LANES : N - LANES] = x_mid.astype(bf16)
+    y = dot_nt(xs[...], dmat[...]).astype(bf16)
     zacc[...] = dot(y, dmat[:, :N])
 
     def end_columns(flat, width):
@@ -614,21 +654,23 @@
 
     @pl.when(is_hub)
     def _():
-        qc_near[...] = near_strips(
-            zacc[...].astype(bf16), 2 * ROWS, row_parts, by_hub(forward, back_row), to_strips
-        )
-        for i, there in ((1, 1), (2, T - 2)):
-            remote(
-                qc_near.at[i], qr_c.at[hub], sc_s.at[3 + i], sc_r.at[2, hub], there
-            ).start()
+        value = turn_rows(zacc[...].astype(bf16), to_strips)
+        qc[...] = value.astype(bf16).reshape(T, ROWS, WIDE)
+
+        def send(there):
+            @pl.when((there > 0) & (there < T - 1))
+            def _():
+                remote(qc.at[there], qr_c.at[hub], sc_s.at[2], sc_r.at[2, hub], there).start()
+
+        each_tile(send)
 
     ring_d = [
-        remote(sp.at[0], drh.at[1], ring_s.at[2], ring_r.at[2], prev),
-        remote(sp.at[1], drh.at[0], ring_s.at[3], ring_r.at[3], nxt),
+        remote(sp.at[0], drh.at[1], ring_s.at[4], ring_r.at[4], prev),
+        remote(sp.at[1], drh.at[0], ring_s.at[5], ring_r.at[5], nxt),
     ]
     ring_late = [
-        remote(late.at[0], late_r.at[1], ring_s.at[4], ring_r.at[4], prev),
-        remote(late.at[1], late_r.at[0], ring_s.at[5], ring_r.at[5], nxt),
+        remote(late.at[0], late_r.at[1], ring_s.at[6], ring_r.at[6], prev),
+        remote(late.at[1], late_r.at[0], ring_s.at[7], ring_r.at[7], nxt),
     ]
 
     def start_spills(value):
@@ -646,7 +688,7 @@
     def _():
         pall_c[t] = pa_c[hub]
         wait_at_hub(pall_c, 1)
-        zacc[...] += gather_rows(MR, row_parts, by_hub(forward, back_row), pall_c, ())
+        zacc[...] += gather_rows(3, MR, pall_c[...].reshape(N, WIDE), ())
 
     ends = dot_nt(spread(arrive_cols(pc, pc_mir, None)), sel)
     zacc[:, :LANES] += ends[:, :LANES]
@@ -657,16 +699,16 @@
 
     def both_ends(value):
         return dot(jnp.concatenate([value[:, :LANES], value[:, N - LANES :]], axis=1), sel)
+
+    @pl.when(is_hub)
+    def _():
+        start_spills(z)
 
     z_ends = both_ends(z).astype(bf16)
     for side in range(2):
         value = dot(bdht[side], z_ends)
         late[side] = jnp.where(quarter == 1 - side, value, 0.0).astype(bf16)
         ring_late[side].start()
-
-    @pl.when(is_hub)
-    def _():
-        start_spills(z)
 
     hub_d = remote(qd.at[1 - hub], qr_d.at[hub], sc_s.at[3], sc_r.at[3, hub], mirror)
 
@@ -693,13 +735,7 @@
 
     @pl.when(is_hub)
     def _():
-        arrived = gather_rows(
-            MH, halo_parts, by_hub(forward, back_halo), None,
-            (
-                (sp[hub], halo_parts, by_hub(back_halo, forward), hub),
-                (drh[hub], halo_parts, by_hub(forward, back_halo), 1 - hub),
-            ),
-        ).astype(bf16)
+        arrived = gather_rows(4, MH, None, (sp[hub], drh[hub])).astype(bf16)
         drh[hub] = arrived
         late_r[hub] = jnp.where(quarter == hub, both_ends(arrived), 0.0).astype(bf16)
 
@@ -727,7 +763,8 @@
         r, c = u // NB, u % NB
         part[u // per_chunk, u % per_chunk] = total[r * 8 : r * 8 + 8, c * LANES : (c + 1) * LANES]
 
-    peers_of_me = [lax.rem(me + i, count) for i in range(1, count)]
+    order = [12, 13, 14, 15, 10, 11, 8, 9, 4, 5, 6, 7, 2, 3, 1] if count == 16 else range(1, count)
+    peers_of_me = [me ^ i for i in order]
     for there in peers_of_me:
         remote(part.at[there], got.at[me], mem_s.at[0], mem_r.at[0], there, "member").start()
     got[me] = part[me]
@@ -746,7 +783,7 @@
         r, c = u // NB, u % NB
         out[r * 8 : r * 8 + 8, c * LANES : (c + 1) * LANES] = done[u // per_chunk, u % per_chunk]
 
-    for copy in ring_a + ring_d + ring_late + [mirror_c]:
+    for copy in ring_a + ring_mid + ring_d + ring_late + [mirror_c]:
         copy.wait_send()
     for i, (there, other, inside) in enumerate((beside[0], middle, beside[1])):
         @pl.when(other & inside)
@@ -759,10 +796,8 @@
     @pl.when(is_hub)
     def _():
         finish_scatter(qw, 0)
-        far = qc.at[pl.ds(0, T - 4)]
+        far = qc.at[pl.ds(0, T - 2)]
         pltpu.make_async_copy(far, far, sc_s.at[2]).wait()
-        for i in (1, 2):
-            remote(qc_near.at[i], qr_c.at[hub], sc_s.at[3 + i], sc_r.at[2, hub], 1).wait_send()
         mirror_b.wait_send()
         hub_d.wait_send()
 
@@ -796,8 +831,8 @@
             pltpu.SMEM(args[4].shape, i32),
             pltpu.SMEM(args[5].shape, i32),
             pltpu.VMEM((MR, N), bf16),
-            pltpu.VMEM((2, MH, N), bf16),
-            pltpu.VMEM((2, MH, N), bf16),
+            pltpu.VMEM((2, 2, MH, WIDE), bf16),
+            pltpu.VMEM((2, 2, MH, WIDE), bf16),
             pltpu.VMEM((2, ROWS, WIDE), bf16),
             pltpu.VMEM((T, ROWS, WIDE), bf16),
             pltpu.VMEM((M, ROWS, WIDE), bf16),
@@ -814,7 +849,6 @@
             pltpu.VMEM((2, ROWS, WIDE), bf16),
             pltpu.VMEM((T, ROWS, WIDE), bf16),
             pltpu.VMEM((T, ROWS, WIDE), bf16),
-            pltpu.VMEM((4, ROWS, WIDE), bf16),
             pltpu.VMEM((2, ROWS, WIDE), bf16),
             pltpu.VMEM((2, MH, N), bf16),
             pltpu.VMEM((2, MH, N), bf16),
@@ -832,12 +866,15 @@
             pltpu.VMEM((N, N), bf16),
             pltpu.VMEM((3, WIDE, WIDE), bf16),
             pltpu.VMEM((2, 2 * WIDE + LANES, WIDE), bf16),
+            pltpu.VMEM((2 * WIDE + LANES, WIDE), f32),
+            pltpu.VMEM((2 * WIDE + LANES, LANES), bf16),
+            pltpu.VMEM((6, 2 * MR, WIDE), bf16),
             pltpu.VMEM((count, per_chunk, 8, LANES), f32),
             pltpu.VMEM((count, per_chunk, 8, LANES), f32),
             pltpu.VMEM((per_chunk, 8, LANES), f32),
             pltpu.VMEM((count, per_chunk, 8, LANES), f32),
             dma((6,)),
-            dma((6,)), dma((6,)),
+            dma((8,)), dma((8,)),
             dma((2, 2)), dma((2,)),
             dma((2,)), dma((2,)),
             dma((3,)), dma((3,)),

time: 61.5 us -> 60.3 us (0.980)
  Pallas kernels: 59.7 us -> 58.5 us
    pallas_call x1, Pallas kernels: 59.7 us -> 58.5 us  [per_device(): pl.pallas_call(functools.partial(whole_kernel, T, M, count), out_shape=ja...]
where the time goes in v5:
time: 60.3 us; the launch traced here: 60.1 us
  Pallas kernels  58.5 us (97%)
  local copies, waits for them, and re-layouts  1.62 us (3%)
    pallas_call x1, Pallas kernels, per_device(): pl.pallas_call(functools.partial(whole_kernel, T, M, count), out_shape=ja...  58.5 us
    unnamed x1, local copies, waits for them, and re-layouts  1.62 us

profile of v5, /device:TPU:1, one launch (start us, length us, event | category | flops | bytes accessed | tf_op | source)
XLA Modules:
  0.0 60.1 jit_solution(1731890752793812783)
XLA Ops:
  0.0 58.5 %covariance.1 = f32[96,512]{1,0:T(8,128)} custom-call(bf16[2,6,16,512]{3,2,1,0:T(8,128)(2,1)} %pert_in.1, f32[6,16,512]{2,1,0:T(8,128)} %control_in.1, f32[16,25]{1,0:T(8,128)} %rows_in.1, f32[25,512]{1,0:T(8,128)} %bitcast.5, s32[4,6]{1,0:T(4,128)} %bitcast.6, s32[4,6]{1,0:T(4,128)} %bitcast.7), custom_call_target="tpu_custom_call" | custom-call | tf_op jit(solution)/shard_map/covariance/pallas_call | solution.py:821
  58.5 1.6 %copy.8 = f32[6,16,512]{2,1,0:T(8,128)} copy(f32[6,16,512]{2,1,0:T(8,128)} %bitcast.4) | data formatting | bytes 393216

commit v6 on v5

--- a/solution.py
+++ b/solution.py
@@ -773,15 +773,19 @@
     chunk = got[0]
     for i in range(1, count):
         chunk = chunk + got[i]
-    mine[...] = chunk * (1.0 / (M * count - 1.0))
+    chunk = (chunk * (1.0 / (M * count - 1.0))).reshape(8 * per_chunk, LANES)
+    spare = jnp.zeros((mine.shape[0] - 8 * per_chunk, LANES), f32)
+    mine[...] = jnp.concatenate([chunk, spare], axis=0).astype(bf16)
     for there in peers_of_me:
         remote(mine, done.at[me], mem_s.at[1], mem_r.at[1], there, "member").start()
     done[me] = mine[...]
     finished = done.at[pl.ds(0, count - 1)]
     pltpu.make_async_copy(finished, finished, mem_r.at[1]).wait()
-    for u in range(count * per_chunk):
-        r, c = u // NB, u % NB
-        out[r * 8 : r * 8 + 8, c * LANES : (c + 1) * LANES] = done[u // per_chunk, u % per_chunk]
+    for i in range(count):
+        block = done[i].astype(f32)
+        for k in range(per_chunk):
+            r, c = (i * per_chunk + k) // NB, (i * per_chunk + k) % NB
+            out[r * 8 : r * 8 + 8, c * LANES : (c + 1) * LANES] = block[8 * k : 8 * k + 8]
 
     for copy in ring_a + ring_mid + ring_d + ring_late + [mirror_c]:
         copy.wait_send()
@@ -805,8 +809,8 @@
     def _():
         finish_scatter(qs, 1)
 
-    for i in range(2):
-        pltpu.make_async_copy(others, others, mem_s.at[i]).wait()
+    pltpu.make_async_copy(others, others, mem_s.at[0]).wait()
+    pltpu.make_async_copy(finished, finished, mem_s.at[1]).wait()
 
 
 def per_device(perturbations, control, band_rows, band_cols, edge_peer, edge_flip):
@@ -871,8 +875,8 @@
             pltpu.VMEM((6, 2 * MR, WIDE), bf16),
             pltpu.VMEM((count, per_chunk, 8, LANES), f32),
             pltpu.VMEM((count, per_chunk, 8, LANES), f32),
-            pltpu.VMEM((per_chunk, 8, LANES), f32),
-            pltpu.VMEM((count, per_chunk, 8, LANES), f32),
+            pltpu.VMEM((-(-per_chunk // 2) * 16 + 16 * (per_chunk % 2 == 0), LANES), bf16),
+            pltpu.VMEM((count, -(-per_chunk // 2) * 16 + 16 * (per_chunk % 2 == 0), LANES), bf16),
             dma((6,)),
             dma((8,)), dma((8,)),
             dma((2, 2)), dma((2,)),

time: 60.3 us -> 59.8 us (level)
  no operation moved by 1% of the time
where the time goes in v6:
time: 59.8 us; the launch traced here: 59.6 us
  Pallas kernels  58 us (97%)
  local copies, waits for them, and re-layouts  1.62 us (3%)
    pallas_call x1, Pallas kernels, per_device(): pl.pallas_call(functools.partial(whole_kernel, T, M, count), out_shape=ja...  58 us
    unnamed x1, local copies, waits for them, and re-layouts  1.62 us

profile of v6, /device:TPU:1, one launch (start us, length us, event | category | flops | bytes accessed | tf_op | source)
XLA Modules:
  0.0 59.6 jit_solution(2449601530275025932)
XLA Ops:
  0.0 58.0 %covariance.1 = f32[96,512]{1,0:T(8,128)} custom-call(bf16[2,6,16,512]{3,2,1,0:T(8,128)(2,1)} %pert_in.1, f32[6,16,512]{2,1,0:T(8,128)} %control_in.1, f32[16,25]{1,0:T(8,128)} %rows_in.1, f32[25,512]{1,0:T(8,128)} %bitcast.5, s32[4,6]{1,0:T(4,128)} %bitcast.6, s32[4,6]{1,0:T(4,128)} %bitcast.7), custom_call_target="tpu_custom_call" | custom-call | tf_op jit(solution)/shard_map/covariance/pallas_call | solution.py:825
  58.0 1.6 %copy.8 = f32[6,16,512]{2,1,0:T(8,128)} copy(f32[6,16,512]{2,1,0:T(8,128)} %bitcast.4) | data formatting | bytes 393216
